TPU v7x, 768 devices: a whole 4x8x12 slice. The times are simulated.
768 devices in a mesh: tensor: 24 (over z, core), dp: 32 (over x, y).
Axes of the slice: x: 4, y: 8, z: 12, core: 2. Of those that a mesh axis runs over, the one named last changes fastest.
Arguments:
- gate_pre: bfloat16 [4096, 15360], P('dp', 'tensor'), may hold values from -8 to 8
- up_pre: bfloat16 [4096, 15360], P('dp', 'tensor'), may hold values from -6 to 6
- out_grad: bfloat16 [4096, 6144], P('dp', 'tensor'), may hold values from -6 to 6
- weight_slots: bfloat16 [1728, 128, 128], P('tensor'), may hold values from -0.15625 to 0.15625
- holder_blocks: int32 [1728, 2], P('tensor'), may hold values from 0 to 119, as said below
- holder_live_slots: int32 [576], P('tensor'), may hold values from 2 to 3, as said below
- row_columns: int32 [120, 12], P('tensor'), may hold values from 0 to 47, as said below
Outputs:
- gate_grad: bfloat16 [4096, 15360], P('dp', 'tensor')
- up_grad: bfloat16 [4096, 15360], P('dp', 'tensor')
- weight_grad: bfloat16 [1440, 16384], P('tensor', 'dp')
Inputs may be any that keep to these rules, and one draw needn't show every extreme that they name: `holder_blocks`: slot s of holder h (row h * 72 + s) names a live block (its row block, then its column block, a column that row_columns lists for that row) when it is live by holder_live_slots, and (0, 0) otherwise; a live slot's row block lies among those of tensor index s // 3, that is from (s // 3) * 5 on; every live block is named by exactly one slot. `holder_live_slots`: entry h * 24 + o counts the live slots of holder h for the row blocks of tensor index o; for each o they sum over h to 60; some holder has 3 in every entry. `row_columns`: each row holds 12 distinct column blocks in rising order.
All inputs are finite; a program needn't handle non-finite values.
Results may differ from a plain program's by a relative error of at most 0.022.
Values may be sent and summed in bfloat16 or wider, within the bound.
A program may use at most 64 MiB of HBM per device.

v0:
```python
import jax
import jax.numpy as jnp
from jax import lax
from jax.sharding import PartitionSpec as P

FF = 15360


def gating(gate_pre, up_pre):
    gate_value = gate_pre.astype(jnp.float32)
    sigmoid_gate = jax.nn.sigmoid(gate_value)
    activation = gate_value * sigmoid_gate
    slope_value = sigmoid_gate * (1.0 + gate_value * (1.0 - sigmoid_gate))
    return (activation, slope_value, up_pre.astype(jnp.float32))


def slot_alive_mask(holder_live_slots, total_slot_count):
    width = holder_live_slots.shape[0]
    cap_here = total_slot_count // width
    slot_ids = jnp.arange(total_slot_count, dtype=jnp.int32)
    return slot_ids % cap_here < holder_live_slots[slot_ids // cap_here]


def holder_partial(grad_blocks, weight_slots, holder_blocks, holder_live_slots):
    local_tokens = grad_blocks.shape[0]
    block_size = grad_blocks.shape[2]
    total_slot_count = weight_slots.shape[0]
    alive_flags = slot_alive_mask(holder_live_slots, total_slot_count)
    live_total = jnp.sum(alive_flags.astype(jnp.int32))
    places = jnp.cumsum(alive_flags.astype(jnp.int32)) - 1
    slot_ids = jnp.arange(total_slot_count, dtype=jnp.int32)
    ordering = (
        jnp.zeros((total_slot_count,), jnp.int32)
        .at[jnp.where(alive_flags, places, total_slot_count)]
        .set(slot_ids, mode="drop")
    )
    bundle = 8

    def add_slots(entry_count, partial_value):
        first_slot = entry_count * bundle
        selected_entry = lax.dynamic_slice_in_dim(ordering, first_slot, bundle, 0)
        weights = weight_slots[selected_entry]
        coords = holder_blocks[selected_entry]
        picked = grad_blocks[:, coords[:, 1], :]
        contrib = jnp.einsum("tsk,sjk->tsj", picked, weights, preferred_element_type=jnp.float32)
        active = first_slot + jnp.arange(bundle, dtype=jnp.int32) < live_total
        contrib = jnp.where(active[None, :, None], contrib, 0.0)
        return partial_value.at[:, coords[:, 0], :].add(contrib)

    partial_value = jnp.zeros((local_tokens, FF // block_size, block_size), jnp.float32)
    partial_value = lax.fori_loop(0, (live_total + bundle - 1) // bundle, add_slots, partial_value)
    return partial_value.reshape(local_tokens, FF)


def weight_gradient(hidden, grad_blocks, row_columns):
    local_tokens = hidden.shape[0]
    block_size = grad_blocks.shape[2]
    rows_here, keep_count = row_columns.shape
    hidden_blocks = hidden.reshape(local_tokens, rows_here, block_size)
    picked = grad_blocks[:, row_columns.reshape(-1), :].reshape(
        local_tokens, rows_here, keep_count, block_size
    )
    block_terms = jnp.einsum(
        "tpa,tpkb->pkab", hidden_blocks, picked, preferred_element_type=jnp.float32
    )
    block_terms = block_terms.reshape(rows_here * keep_count, block_size * block_size)
    return lax.psum_scatter(block_terms.astype(jnp.bfloat16), "dp", scatter_dimension=1, tiled=True)


def local(gate_pre, up_pre, out_grad, weight_slots, holder_blocks, holder_live_slots, row_columns):
    full_grad = lax.all_gather(out_grad, "tensor", axis=1, tiled=True)
    local_tokens = full_grad.shape[0]
    block_size = weight_slots.shape[1]
    grad_blocks = full_grad.reshape(local_tokens, -1, block_size)
    activation, slope_value, up_value = gating(gate_pre, up_pre)
    hidden = (activation * up_value).astype(jnp.bfloat16)
    dense = holder_partial(grad_blocks, weight_slots, holder_blocks, holder_live_slots)
    hidden_grad = lax.psum_scatter(
        dense.astype(jnp.bfloat16), "tensor", scatter_dimension=1, tiled=True
    ).astype(jnp.float32)
    weight_grad = weight_gradient(hidden, grad_blocks, row_columns)
    gate_grad = (hidden_grad * up_value * slope_value).astype(jnp.bfloat16)
    up_grad = (hidden_grad * activation).astype(jnp.bfloat16)
    return (gate_grad, up_grad, weight_grad)


def solution(mesh):
    placed = (
        P("dp", "tensor"),
        P("dp", "tensor"),
        P("dp", "tensor"),
        P("tensor", None, None),
        P("tensor", None),
        P("tensor"),
        P("tensor", None),
    )
    return jax.shard_map(
        local,
        mesh=mesh,
        in_specs=placed,
        out_specs=(P("dp", "tensor"), P("dp", "tensor"), P("tensor", "dp")),
        check_vma=False,
    )
```

profile of v0, /device:TPU:1, one launch (start us, length us, event | category | flops | bytes accessed | tf_op | source)
XLA Modules:
  0.0 487.5 jit_solution(6581681672548813339)
XLA Ops:
  7.2 1.6 copy.30
  9.0 1.2 gather_fusion.3
  10.3 0.6 fusion.24
  11.8 0.8 copy.31
  12.7 0.8 scatter_custom_fusion.1
  13.5 65.4 %all-gather.2.cloned.1.call-done = bf16[128,6144]{0,1:T(8,128)(2,1)} async-done(((bf16[128,256]{0,1:T(8,128)(2,1)}), bf16[128,6144]{0,1:T(8,128)(2,1)}) %all-gather.2.cloned.1.call-update) | async-done | bytes 1572880 | tf_op jit(solution)/shard_map/all_gather | solution.py:71
  78.9 1.9 copy.32
  80.8 4.1 broadcast_in_dim.29
  84.9 60.6 %while.10 = (s32[]{:T(128)}, f32[128,120,128]{2,0,1:T(8,128)}, s32[]{:T(128)}, s32[72]{0:T(128)S(1)}, s32[72,2]{1,0:T(8,128)S(1)}, /*index=5*/s32[]{:T(128)}, bf...) while((s32[]{:T(128)}, f32[128,120,128]{2,0,1:T(8,128)}, ...), condition=%wide.region_5.6_spmd, body=%wide.region_3.5_spmd.sunk | while | flops 33818716 | bytes 4727487 | solution.py:51
  84.9 0.6 gather_fusion
  85.7 0.6 gather_fusion.2
  86.3 2.3 gather_fusion.1
  88.6 0.7 add_compare_fusion.2
  89.7 2.7 scatter_fusion
  92.5 0.6 gather_fusion
  93.3 0.6 gather_fusion.2
  93.9 2.3 gather_fusion.1
  96.1 0.7 add_compare_fusion.2
  97.3 2.7 scatter_fusion
  100.0 0.6 gather_fusion
  100.8 0.6 gather_fusion.2
  101.4 2.3 gather_fusion.1
  103.7 0.7 add_compare_fusion.2
  104.8 2.7 scatter_fusion
  107.6 0.6 gather_fusion
  108.3 0.6 gather_fusion.2
  109.0 2.3 gather_fusion.1
  111.2 0.7 add_compare_fusion.2
  112.4 2.7 scatter_fusion
  115.2 0.6 gather_fusion
  115.9 0.6 gather_fusion.2
  116.5 2.3 gather_fusion.1
  118.8 0.7 add_compare_fusion.2
  120.0 2.7 scatter_fusion
  122.8 0.6 gather_fusion
  123.5 0.6 gather_fusion.2
  124.1 2.3 gather_fusion.1
  126.4 0.7 add_compare_fusion.2
  127.5 2.7 scatter_fusion
  130.3 0.6 gather_fusion
  131.1 0.6 gather_fusion.2
  131.7 2.3 gather_fusion.1
  133.9 0.7 add_compare_fusion.2
  135.1 2.7 scatter_fusion
  137.9 0.6 gather_fusion
  138.7 0.6 gather_fusion.2
  139.3 2.3 gather_fusion.1
  141.5 0.7 add_compare_fusion.2
  142.7 2.7 scatter_fusion
  145.4 6.1 %convert_element_type.48 = bf16[128,120,128]{2,0,1:T(8,128)(2,1)} convert(f32[128,120,128]{2,0,1:T(8,128)} %get-tuple-element.46) | non-fusion elementwise | flops 1966080 | bytes 11796480 | tf_op jit(solution)/shard_map/convert_element_type | solution.py:79
  151.6 6.3 %copy.33 = bf16[128,120,128]{0,2,1:T(8,128)(2,1)} copy(bf16[128,120,128]{2,0,1:T(8,128)(2,1)} %convert_element_type.48) | data formatting | bytes 7864320 | tf_op jit(solution)/shard_map/convert_element_type | solution.py:79
  157.9 0.8 copy-done.3
  158.8 0.8 copy.34
  159.6 0.8 copy.35
  160.5 0.9 gather_fusion.4
  161.4 87.5 %reduce-scatter.3.cloned.1.call-done = bf16[128,640]{0,1:T(8,128)(2,1)} async-done(((bf16[128,15360]{0,1:T(8,128)(2,1)}), bf16[128,640]{0,1:T(8,128)(2,1)}) %reduce-scatter.3.cloned.1.call-update) | async-done | bytes 163856 | tf_op jit(solution)/shard_map/reduce_scatter | solution.py:78
  249.0 2.0 fusion.7
  251.0 2.1 convert_bitcast_fusion
  253.1 2.9 copy.39
  256.2 2.8 copy.46
  259.0 0.9 copy-done.2
  259.9 0.8 copy.40
  260.7 0.8 copy.41
  261.5 219.4 %reduce-scatter.5.cloned.1.call-done = bf16[60,512]{1,0:T(8,128)(2,1)} async-done(((bf16[60,16384]{1,0:T(8,128)(2,1)}), bf16[60,512]{1,0:T(8,128)(2,1)}) %reduce-scatter.5.cloned.1.call-update) | async-done | bytes 61456 | tf_op jit(solution)/shard_map/reduce_scatter | solution.py:67
  (75 shorter events, 7.2 us)
Async XLA Ops:
  7.2 1.8 copy-start
  7.2 71.7 %all-gather.2.cloned.1.call-start = ((), (), s32[]{:S(2)}) async-start(), calls=%async_computation.2 | async-start | bytes 1638400 | tf_op jit(solution)/shard_map/all_gather | solution.py:71
  8.8 240.1 %reduce-scatter.3.cloned.1.call-start = ((), (), s32[]{:S(2)}) async-start(), calls=%async_computation.3 | async-start | bytes 4096000 | tf_op jit(solution)/shard_map/reduce_scatter | solution.py:78
  157.8 0.9 copy-start.3
  157.8 1.7 copy-start.4
  157.8 2.5 copy-start.5
  157.9 323.1 %reduce-scatter.5.cloned.1.call-start = ((), (), s32[]{:S(2)}) async-start(), calls=%async_computation.4 | async-start | bytes 2162688 | tf_op jit(solution)/shard_map/reduce_scatter | solution.py:67
  259.0 0.9 copy-start.2
  259.0 1.7 copy-start.1
Sparse Core Ops, SparseCore 0:
  11.0 67.8 all-gather.1
  158.0 90.9 reduce-scatter.2
  259.1 221.7 reduce-scatter.4
where the time goes:
time: 492 us; the launch traced here: 487 us
  waiting for transfers between devices  372 us (76%)
  local copies, waits for them, and re-layouts  57.5 us (12%)
  other arithmetic  38.1 us (8%)
  between operations  14.5 us (3%)
    reduce_scatter x1, waiting for transfers between devices, weight_gradient(): lax.psum_scatter(block_terms.astype(jnp.bfloat16), 'dp', scatter_dimensio...  219 us
    reduce_scatter x1, waiting for transfers between devices, local(): lax.psum_scatter(dense.astype(jnp.bfloat16), 'tensor', scatter_dimension=...  87.5 us
    all_gather x1, waiting for transfers between devices, local(): full_grad = lax.all_gather(out_grad, 'tensor', axis=1, tiled=True)  65.4 us
    scatter-add x8, other arithmetic, add_slots(): return partial_value.at[:, coords[:, 0], :].add(contrib)  21.5 us
    gather x8, local copies, waits for them, and re-layouts, add_slots(): weights = weight_slots[selected_entry]  18.1 us
  transfers between devices with their start and end apart: 3, of which 3 were waited for; matrix products, arithmetic and copies ran while one was open for 2% of the time, Pallas kernels for 0%

commit v1 on v0

v1 whole, which is shorter than its diff:
```python
import jax
import jax.numpy as jnp
from jax import lax
from jax.experimental import pallas as pl
from jax.experimental.pallas import tpu as pltpu
from jax.sharding import PartitionSpec as P

MESH = pl.DeviceIdType.MESH
NX, NY, NZ = 4, 8, 12
NT = 2 * NZ
RZ, RY = NZ // 2, NY // 2
ROWS, KEEP, B = 5, 12, 128
HALF = KEEP // 2 * B
BF, F32 = jnp.bfloat16, jnp.float32
CUT = 128
NROW = ROWS * KEEP * 4


def kernel(
    gate, up, og, w_hbm, hb, live, rc,
    gg, ug, wg,
    og_all, slab, msg, recv, comm_x, w_all, act, slope_up, hid_t, part, buf_x, fin_x, snd_x, yin, snd_y, rcv_y,
    slab_sem, z_send, z_recv, s_send, s_recv, a_send, a_recv, gx_send, gx_recv, gy_send, gy_recv,
    rx_send, rx_recv, ry_send, ry_recv,
):
    t, d = lax.axis_index("tensor"), lax.axis_index("dp")
    z, c = lax.div(t, 2), lax.rem(t, 2)
    x, y = lax.div(d, NY), lax.rem(d, NY)

    def zdev(k):
        return {"tensor": lax.rem(z + k + NZ, NZ) * 2 + c}

    def xdev(k):
        return {"dp": lax.rem(x + k + NX, NX) * NY + y}

    def ydev(k):
        return {"dp": x * NY + lax.rem(y + k + NY, NY)}

    sibling = {"tensor": z * 2 + (1 - c)}

    def copy(src, dst, ss, rs, dev):
        return pltpu.make_async_remote_copy(
            src_ref=src, dst_ref=dst, send_sem=ss, recv_sem=rs, device_id=dev, device_id_type=MESH
        )

    slab_copy = pltpu.make_async_copy(w_hbm.at[:, pl.ds(pl.multiple_of(y * 16, 16), 16), :], slab, slab_sem)
    slab_copy.start()

    barrier = pltpu.get_barrier_semaphore()

    def greet(s, carry):
        pl.semaphore_signal(barrier, inc=1, device_id={"tensor": lax.rem(t + s, NT)}, device_id_type=MESH)
        return carry

    lax.fori_loop(1, NT, greet, 0)
    for k in (1, 2, 3):
        pl.semaphore_signal(barrier, inc=1, device_id=xdev(k), device_id_type=MESH)
    for k in (1, -1):
        pl.semaphore_signal(barrier, inc=1, device_id=ydev(k), device_id_type=MESH)
    pend = []

    og_all[2 * t] = og[:, :B]
    og_all[2 * t + 1] = og[:, B:]
    pl.semaphore_wait(barrier, NT - 1 + 3 + 2)

    def zslot(k, cc, h):
        return 2 * (lax.rem(z + k + NZ, NZ) * 2 + cc) + h

    def chunks(s):
        if s < RZ:
            return [(0, 0), (1, 0), (0, 1), (1, 1)]
        return [(0, 0), (1, 1)]

    def z_start(s, e, h):
        sg = 1 if e == 0 else -1
        slot = og_all.at[zslot(-sg * (s - 1), c, h)]
        cp = copy(slot, slot, z_send.at[e, s - 1, h], z_recv.at[e, s - 1, h], zdev(sg))
        cp.start()
        pend.append(cp)

    def sib_start(s, e, h):
        sg = 1 if e == 0 else -1
        slot = og_all.at[zslot(-sg * s, c, h)]
        cp = copy(slot, slot, s_send.at[e, s, h], s_recv.at[e, s, h], sibling)
        cp.start()
        pend.append(cp)

    def sib_wait(s, e, h):
        sg = 1 if e == 0 else -1
        slot = og_all.at[zslot(-sg * s, 1 - c, h)]
        copy(slot, slot, s_send.at[e, s, h], s_recv.at[e, s, h], sibling).wait_recv()

    def z_step(s):
        for e, h in chunks(s):
            sg = 1 if e == 0 else -1
            slot = og_all.at[zslot(-sg * s, c, h)]
            copy(slot, slot, z_send.at[e, s - 1, h], z_recv.at[e, s - 1, h], zdev(sg)).wait_recv()
            if s < RZ and (e, h) in chunks(s + 1):
                z_start(s + 1, e, h)
            sib_start(s, e, h)

    for e, h in chunks(1):
        z_start(1, e, h)
    for h in (0, 1):
        sib_start(0, 0, h)

    slab_copy.wait()
    r_out = lax.broadcasted_iota(jnp.int32, (64, 192), 0)
    r_in = lax.broadcasted_iota(jnp.int32, (64, 192), 1)
    q = lax.rem(r_out, 16)
    pick = (
        (lax.div(r_out, 16) == lax.div(r_in, 48))
        & (lax.div(q, 4) == lax.div(lax.rem(r_in, 48), 16))
        & (q < 12)
        & (x * 4 + lax.rem(q, 4) == lax.rem(r_in, 16))
    )
    pick = jnp.where(pick, 1.0, 0.0).astype(BF)
    row16 = lax.broadcasted_iota(jnp.int32, (16, B), 0)

    def make_msg(m, carry):
        rows = slab[pl.ds(m * 12, 12)].reshape(192, B)
        picked = jnp.dot(pick, rows, preferred_element_type=F32)
        for u in range(4):
            o = m * 4 + u
            tile = picked[16 * u : 16 * u + 16]
            for s in range(3):
                key = (hb[o * 3 + s, 0] - o * ROWS) * 48 + hb[o * 3 + s, 1]
                key = jnp.where(s < live[o], key, -1).astype(F32)
                tile = jnp.where(row16 == 12 + s, key, tile)
            msg[o] = tile.astype(BF)
        return carry

    lax.fori_loop(0, NT // 4, make_msg, 0)
    recv[t] = msg[t]

    def a_copy(s):
        o = lax.rem(t + s, NT)
        return copy(msg.at[o], recv.at[t], a_send.at[s], a_recv.at[t], {"tensor": o})

    def a_start(s, carry):
        a_copy(s).start()
        return carry

    lax.fori_loop(1, NT, a_start, 0)

    for i in range(ROWS):
        g = gate[:, i * B : (i + 1) * B].astype(F32)
        u = up[:, i * B : (i + 1) * B].astype(F32)
        sig = 1.0 / (1.0 + jnp.exp(-g))
        a = g * sig
        act[:, i * B : (i + 1) * B] = a
        slope_up[:, i * B : (i + 1) * B] = u * (sig * (1.0 + g * (1.0 - sig)))
        hid_t[i] = (a * u).T.astype(BF)

    lane = lax.broadcasted_iota(jnp.int32, (8, 2 * B), 1)
    block_of = lax.div(lane, 4)
    keycol = jnp.full((8, 2 * B), -100.0, F32)
    for n in range(ROWS * KEEP):
        v = ((n // KEEP) * 48 + rc[n // KEEP, n % KEEP]) * 4
        keycol = jnp.where(block_of == n, v.astype(F32), keycol)
    keycol = (keycol + lax.rem(lane, 4).astype(F32))[0:1]

    z_step(1)
    z_step(2)

    def a_wait(s, carry):
        h = lax.rem(t + s, NT)
        copy(msg.at[h], recv.at[h], a_send.at[s], a_recv.at[h], {"tensor": h}).wait_recv()
        return carry

    lax.fori_loop(1, NT, a_wait, 0)

    got = recv[...]
    gotf = got.astype(F32)
    rr = lax.broadcasted_iota(jnp.int32, (NT, 16, B), 1)
    keyrow = jnp.where(
        rr < 4, gotf[:, 12:13, :], jnp.where(rr < 8, gotf[:, 13:14, :], jnp.where(rr < 12, gotf[:, 14:15, :], -1000.0))
    )
    keyrow = (keyrow * 4.0 + lax.rem(rr, 4).astype(F32)).reshape(NT * 16, B)
    got = got.reshape(NT * 16, B)
    for v in range(2):
        hot = jnp.where(keyrow == keycol[:, v * B : (v + 1) * B], 1.0, 0.0).astype(BF)
        res = lax.dot_general(hot, got, (((0,), (0,)), ((), ())), preferred_element_type=F32).astype(BF)
        n_tiles = 8 if v == 0 else 7
        comm_x[x, 8 * v : 8 * v + n_tiles] = res[: 16 * n_tiles].reshape(n_tiles, 16, B)

    for k in (1, 3, 2):
        cp = copy(comm_x.at[x], comm_x.at[x], gx_send.at[k - 1], gx_recv.at[k - 1], xdev(k))
        cp.start()
        pend.append(cp)

    z_step(3)
    z_step(4)

    for k in (1, 3, 2):
        src = comm_x.at[lax.rem(x - k + NX, NX)]
        copy(src, src, gx_send.at[k - 1], gx_recv.at[k - 1], xdev(k)).wait_recv()
    p_out = lax.broadcasted_iota(jnp.int32, (64, 64), 0)
    p_in = lax.broadcasted_iota(jnp.int32, (64, 64), 1)
    swap = (
        (lax.div(p_out, 16) == lax.rem(lax.div(p_in, 4), 4))
        & (lax.rem(lax.div(p_out, 4), 4) == lax.div(p_in, 16))
        & (lax.rem(p_out, 4) == lax.rem(p_in, 4))
    )
    swap = jnp.where(swap, 1.0, 0.0).astype(BF)
    for g in range(15):
        res = jnp.dot(swap, comm_x[:, g].reshape(64, B), preferred_element_type=F32).astype(BF)
        for u in range(4):
            n = 4 * g + u
            i, k = n // KEEP, n % KEEP
            w_all[y, k // 6, i, :, (k % 6) * B : (k % 6 + 1) * B] = res[16 * u : 16 * u + 16]

    def y_chunks(s):
        if s < RY:
            return [(0, 0), (1, 1), (0, 1), (1, 0)]
        return [(0, 0), (1, 1)]

    def gy_slot(k, h):
        return w_all.at[lax.rem(y + k + NY, NY), h]

    def gy_start(s, e, h):
        sg = 1 if e == 0 else -1
        slot = gy_slot(-sg * (s - 1), h)
        cp = copy(slot, slot, gy_send.at[e, s - 1, h], gy_recv.at[e, s - 1, h], ydev(sg))
        cp.start()
        pend.append(cp)

    def gy_step(s):
        for e, h in y_chunks(s):
            sg = 1 if e == 0 else -1
            slot = gy_slot(-sg * s, h)
            copy(slot, slot, gy_send.at[e, s - 1, h], gy_recv.at[e, s - 1, h], ydev(sg)).wait_recv()
            if s < RY and (e, h) in y_chunks(s + 1):
                gy_start(s + 1, e, h)

    for e, h in y_chunks(1):
        gy_start(1, e, h)

    z_step(5)
    z_step(6)
    for h in (0, 1):
        sib_wait(0, 0, h)
    for s in range(1, RZ + 1):
        for e, h in chunks(s):
            sib_wait(s, e, h)

    def products(h):
        def one(i, carry):
            for p in range(3):
                k = h * 6 + 2 * p
                pair = jnp.concatenate([og_all[rc[i, k]], og_all[rc[i, k + 1]]], axis=1)
                res = jnp.dot(hid_t[i], pair, preferred_element_type=F32).astype(BF)
                part[:, h, i, :, p * 256 : (p + 1) * 256] = res.reshape(NX, 32, 256)
            return carry

        lax.fori_loop(0, ROWS, one, 0)

    def xi(k):
        return lax.rem(x + k + NX, NX)

    def rx(e, j, src, dst):
        return copy(src, dst, rx_send.at[e, j], rx_recv.at[e, j], xdev(1 if e == 0 else -1))

    def rx_start(*args):
        cp = rx(*args)
        cp.start()
        pend.append(cp)

    products(0)
    rx_start(0, 0, part.at[xi(2), 0], buf_x.at[0])
    rx_start(1, 1, part.at[xi(-1), 0], fin_x.at[1, 0])
    products(1)
    rx_start(1, 0, part.at[xi(2), 1], buf_x.at[1])
    rx_start(0, 1, part.at[xi(1), 1], fin_x.at[0, 1])
    gy_step(1)
    for e in (0, 1):
        rx(e, 0, part.at[xi(2), e], buf_x.at[e]).wait_recv()
        mine = part[xi(1 if e == 0 else -1), e].astype(F32)
        snd_x[e] = (mine + buf_x[e].astype(F32)).astype(BF)
        rx_start(e, 2, snd_x.at[e], fin_x.at[e, e])
    gy_step(2)
    gy_step(3)
    gy_step(4)

    def hidden_grad(i, carry):
        total = jnp.zeros((B, B), F32)
        for h in range(2):
            left = jnp.concatenate([og_all[rc[i, h * 6 + k]] for k in range(6)], axis=1)
            right = w_all[:, h, i].reshape(B, HALF)
            total = total + lax.dot_general(
                left, right, (((1,), (1,)), ((), ())), preferred_element_type=F32
            )
        cols = pl.ds(pl.multiple_of(i * B, B), B)
        gg[:, cols] = (total * slope_up[:, cols]).astype(BF)
        ug[:, cols] = (total * act[:, cols]).astype(BF)
        return carry

    lax.fori_loop(0, ROWS, hidden_grad, 0)

    for e in (0, 1):
        rx(e, 1, part.at[xi(1), 1 - e], fin_x.at[e, 1 - e]).wait_recv()
        rx(e, 2, snd_x.at[e], fin_x.at[e, e]).wait_recv()
    low = lax.broadcasted_iota(jnp.int32, (4, 8, B), 1) < 4
    for h in range(2):
        for i in range(ROWS):
            own = part[x, h, i].astype(F32) + fin_x[0, h, i].astype(F32) + fin_x[1, h, i].astype(F32)
            own = own.reshape(4, 8, HALF)
            for p in range(3):
                a0 = own[:, :, 2 * p * B : (2 * p + 1) * B]
                a1 = own[:, :, (2 * p + 1) * B : (2 * p + 2) * B]
                d0 = jnp.where(low, a0, pltpu.roll(a1, 4, 1))
                d1 = jnp.where(low, pltpu.roll(a0, 4, 1), a1)
                first = (i * KEEP + h * 6 + 2 * p) * 4
                yin[:, 0, first : first + 8, :] = d0
                yin[:, 1, first : first + 8, :] = d1

    span = [pl.ds(0, CUT), pl.ds(CUT, NROW - CUT)]

    def yblock(k, h):
        yy = lax.rem(y + k + NY, NY)
        return yin[lax.div(yy, 2), lax.rem(yy, 2), span[h], :]

    def ry(s, e, h):
        return copy(
            snd_y.at[e, s - 1, span[h], :], rcv_y.at[e, s - 1, span[h], :],
            ry_send.at[e, s - 1, h], ry_recv.at[e, s - 1, h], ydev(1 if e == 0 else -1),
        )

    for s in range(1, RY + 1):
        for e, h in ([(0, 0), (1, 1)] if s == 1 else [(0, 1), (1, 0), (0, 0), (1, 1)] if s == 2 else [(0, 0), (1, 1), (0, 1), (1, 0)]):
            sg = 1 if e == 0 else -1
            v = yblock(sg * (RY + 1 - s), h)
            if s > 2 or (s == 2 and e == h):
                ry(s - 1, e, h).wait_recv()
                v = v + rcv_y[e, s - 2, span[h], :].astype(F32)
            snd_y[e, s - 1, span[h], :] = v.astype(BF)
            cp = ry(s, e, h)
            cp.start()
            pend.append(cp)
    for h in (0, 1):
        for e in (0, 1):
            ry(RY, e, h).wait_recv()
        v = yblock(0, h) + rcv_y[0, RY - 1, span[h], :].astype(F32) + rcv_y[1, RY - 1, span[h], :].astype(F32)
        wg[span[h], :] = v.astype(BF)

    def a_done(s, carry):
        a_copy(s).wait_send()
        return carry

    lax.fori_loop(1, NT, a_done, 0)
    for cp in pend:
        cp.wait_send()


def local(gate_pre, up_pre, out_grad, weight_slots, holder_blocks, holder_live_slots, row_columns):
    vmem = pl.BlockSpec(memory_space=pltpu.VMEM)
    smem = pl.BlockSpec(memory_space=pltpu.SMEM)
    dma = pltpu.SemaphoreType.DMA
    gate_grad, up_grad, weight_grad = pl.pallas_call(
        kernel,
        out_shape=(
            jax.ShapeDtypeStruct(gate_pre.shape, BF),
            jax.ShapeDtypeStruct(gate_pre.shape, BF),
            jax.ShapeDtypeStruct((NROW, B), BF),
        ),
        in_specs=[vmem, vmem, vmem, pl.BlockSpec(memory_space=pl.ANY), smem, smem, smem],
        out_specs=(vmem, vmem, vmem),
        scratch_shapes=[
            pltpu.VMEM((2 * NT, B, B), BF),
            pltpu.VMEM((3 * NT, 16, B), BF),
            pltpu.VMEM((NT, 16, B), BF),
            pltpu.VMEM((NT, 16, B), BF),
            pltpu.VMEM((NX, 15, 16, B), BF),
            pltpu.VMEM((NY, 2, ROWS, 16, HALF), BF),
            pltpu.VMEM((B, ROWS * B), F32),
            pltpu.VMEM((B, ROWS * B), F32),
            pltpu.VMEM((ROWS, B, B), BF),
            pltpu.VMEM((NX, 2, ROWS, 32, HALF), BF),
            pltpu.VMEM((2, ROWS, 32, HALF), BF),
            pltpu.VMEM((2, 2, ROWS, 32, HALF), BF),
            pltpu.VMEM((2, ROWS, 32, HALF), BF),
            pltpu.VMEM((NY // 2, 2, NROW, B), F32),
            pltpu.VMEM((2, RY, NROW, B), BF),
            pltpu.VMEM((2, RY, NROW, B), BF),
            dma,
            dma((2, RZ, 2)), dma((2, RZ, 2)),
            dma((2, RZ + 1, 2)), dma((2, RZ + 1, 2)),
            dma((NT,)), dma((NT,)),
            dma((3,)), dma((3,)),
            dma((2, RY, 2)), dma((2, RY, 2)),
            dma((2, 3)), dma((2, 3)),
            dma((2, RY, 2)), dma((2, RY, 2)),
        ],
        compiler_params=pltpu.CompilerParams(
            collective_id=0, has_side_effects=True, vmem_limit_bytes=40 * 1024 * 1024
        ),
        cost_estimate=pl.CostEstimate(flops=600_000_000, bytes_accessed=4_000_000, transcendentals=82_000),
    )(gate_pre, up_pre, out_grad, weight_slots, holder_blocks, holder_live_slots, row_columns)
    return gate_grad, up_grad, weight_grad.reshape(ROWS * KEEP, 4 * B)


def solution(mesh):
    placed = (
        P("dp", "tensor"),
        P("dp", "tensor"),
        P("dp", "tensor"),
        P("tensor", None, None),
        P("tensor", None),
        P("tensor"),
        P("tensor", None),
    )
    return jax.shard_map(
        local,
        mesh=mesh,
        in_specs=placed,
        out_specs=(P("dp", "tensor"), P("dp", "tensor"), P("tensor", "dp")),
        check_vma=False,
    )
```

time: 492 us -> 92.6 us (0.19)
  the two profiles are of different devices: /device:TPU:1 before, /device:TPU:10 now
where the time goes in v1:
time: 92.6 us; the launch traced here: 92.3 us
  Pallas kernels  83.2 us (90%)
  local copies, waits for them, and re-layouts  8.45 us (9%)
    pallas_call x1, Pallas kernels, local(): pl.pallas_call(kernel, out_shape=(jax.ShapeDtypeStruct(gate_pre.shape, BF...  83.2 us
    unnamed x15, local copies, waits for them, and re-layouts  7.77 us

profile of v1, /device:TPU:10, one launch (start us, length us, event | category | flops | bytes accessed | tf_op | source)
XLA Modules:
  0.0 92.3 jit_solution(8558165596503257436)
XLA Ops:
  0.6 0.8 copy.10.hb
  1.4 0.0 copy-start
  1.4 1.7 %copy-done = bf16[72,128,128]{2,1,0:T(8,128)(2,1)S(1)} copy-done((bf16[72,128,128]{2,1,0:T(8,128)(2,1)S(1)}, bf16[72,128,128]{2,1,0:T(8,128)(2,1)}, u32[]{:S(2)}) %copy-start) | copy-done | bytes 2359320
  3.1 0.0 copy-start.1
  3.1 0.9 copy-done.1
  4.0 0.0 copy-start.2
  4.0 0.9 copy-done.2
  4.9 0.0 copy-start.3
  4.9 0.8 copy-done.3
  5.7 0.0 copy-start.4
  5.7 0.7 copy-done.4
  6.4 0.0 copy-start.5
  6.4 0.7 copy-done.5
  7.1 83.2 %shard_map.94 = (bf16[128,640]{1,0:T(8,128)(2,1)S(1)}, bf16[128,640]{1,0:T(8,128)(2,1)S(1)}, bf16[240,128]{1,0:T(8,128)(2,1)S(1)}) custom-call(bf16[128,640]{1,0:T(8,128)(2,1)S(1)} %copy-done.1, bf16[128,640]{1,0:T(8,128)(2,1)S(1)} %copy-done.2, bf16[128,256]{1,0:T(8,128)(2,1)S(1)} %copy-done.3, bf16[72,128,128]{2,1,0:T(8,128)(2,1)S(1)} %copy-done, ...), custom_call_target="tpu_custom_call" | custom-call | flops 600000000 | bytes 4000000 | tf_op jit(solution)/shard_map/pallas_call | solution.py:359
  90.2 0.7 reshape.9
  90.9 0.7 copy.13
  91.6 0.7 copy.14
Async XLA Ops:
  1.4 1.7 %copy-start = (bf16[72,128,128]{2,1,0:T(8,128)(2,1)S(1)}, bf16[72,128,128]{2,1,0:T(8,128)(2,1)}, u32[]{:S(2)}) copy-start(bf16[72,128,128]{2,1,0:T(8,128)(2,1)} %w_hbm.1) | copy-start | bytes 7077892
  3.1 0.9 copy-start.1
  4.0 0.9 copy-start.2
  4.9 0.8 copy-start.3
  5.7 0.7 copy-start.4
  6.4 0.7 copy-start.5

commit v2 on v1

--- a/solution.py
+++ b/solution.py
@@ -17,10 +17,11 @@
 
 
 def kernel(
-    gate, up, og, w_hbm, hb, live, rc,
-    gg, ug, wg,
+    gate_hbm, up_hbm, og_hbm, w_hbm, hb_hbm, live_hbm, rc_hbm,
+    gg_hbm, ug_hbm, wg_hbm,
+    gate, up, og, hb, live, rc, gg, ug, wg,
     og_all, slab, msg, recv, comm_x, w_all, act, slope_up, hid_t, part, buf_x, fin_x, snd_x, yin, snd_y, rcv_y,
-    slab_sem, z_send, z_recv, s_send, s_recv, a_send, a_recv, gx_send, gx_recv, gy_send, gy_recv,
+    in_sem, out_sem, z_send, z_recv, s_send, s_recv, a_send, a_recv, gx_send, gx_recv, gy_send, gy_recv,
     rx_send, rx_recv, ry_send, ry_recv,
 ):
     t, d = lax.axis_index("tensor"), lax.axis_index("dp")
@@ -43,8 +44,15 @@
             src_ref=src, dst_ref=dst, send_sem=ss, recv_sem=rs, device_id=dev, device_id_type=MESH
         )
 
-    slab_copy = pltpu.make_async_copy(w_hbm.at[:, pl.ds(pl.multiple_of(y * 16, 16), 16), :], slab, slab_sem)
-    slab_copy.start()
+    fetch = [
+        pltpu.make_async_copy(src, dst, in_sem.at[n])
+        for n, (src, dst) in enumerate([
+            (og_hbm, og), (w_hbm.at[:, pl.ds(pl.multiple_of(y * 16, 16), 16), :], slab), (hb_hbm, hb),
+            (live_hbm, live), (rc_hbm, rc), (gate_hbm, gate), (up_hbm, up),
+        ])
+    ]
+    for cp in fetch:
+        cp.start()
 
     barrier = pltpu.get_barrier_semaphore()
 
@@ -59,6 +67,7 @@
         pl.semaphore_signal(barrier, inc=1, device_id=ydev(k), device_id_type=MESH)
     pend = []
 
+    fetch[0].wait()
     og_all[2 * t] = og[:, :B]
     og_all[2 * t + 1] = og[:, B:]
     pl.semaphore_wait(barrier, NT - 1 + 3 + 2)
@@ -68,15 +77,20 @@
 
     def chunks(s):
         if s < RZ:
-            return [(0, 0), (1, 0), (0, 1), (1, 1)]
+            return [(0, 0), (1, 1), (0, 1), (1, 0)]
         return [(0, 0), (1, 1)]
 
-    def z_start(s, e, h):
+    def z_copy(s, k, e, h):
         sg = 1 if e == 0 else -1
-        slot = og_all.at[zslot(-sg * (s - 1), c, h)]
-        cp = copy(slot, slot, z_send.at[e, s - 1, h], z_recv.at[e, s - 1, h], zdev(sg))
-        cp.start()
-        pend.append(cp)
+        slot = og_all.at[zslot(-sg * s, c, h)]
+        return copy(slot, slot, z_send.at[e, s + k - 1, h], z_recv.at[e, s + k - 1, h], zdev(sg * k))
+
+    def z_start(s, e, h, ks=(2, 1)):
+        for k in ks:
+            if (e, h) in chunks(s + k):
+                cp = z_copy(s, k, e, h)
+                cp.start()
+                pend.append(cp)
 
     def sib_start(s, e, h):
         sg = 1 if e == 0 else -1
@@ -95,16 +109,18 @@
             sg = 1 if e == 0 else -1
             slot = og_all.at[zslot(-sg * s, c, h)]
             copy(slot, slot, z_send.at[e, s - 1, h], z_recv.at[e, s - 1, h], zdev(sg)).wait_recv()
-            if s < RZ and (e, h) in chunks(s + 1):
-                z_start(s + 1, e, h)
+            if s in (2, 4):
+                z_start(s, e, h)
             sib_start(s, e, h)
 
-    for e, h in chunks(1):
-        z_start(1, e, h)
+    for k in (2, 1):
+        for e, h in chunks(1):
+            z_start(0, e, h, (k,))
     for h in (0, 1):
         sib_start(0, 0, h)
 
-    slab_copy.wait()
+    for cp in fetch[1:5]:
+        cp.wait()
     r_out = lax.broadcasted_iota(jnp.int32, (64, 192), 0)
     r_in = lax.broadcasted_iota(jnp.int32, (64, 192), 1)
     q = lax.rem(r_out, 16)
@@ -124,7 +140,7 @@
             o = m * 4 + u
             tile = picked[16 * u : 16 * u + 16]
             for s in range(3):
-                key = (hb[o * 3 + s, 0] - o * ROWS) * 48 + hb[o * 3 + s, 1]
+                key = (hb[0, o * 3 + s] - o * ROWS) * 48 + hb[1, o * 3 + s]
                 key = jnp.where(s < live[o], key, -1).astype(F32)
                 tile = jnp.where(row16 == 12 + s, key, tile)
             msg[o] = tile.astype(BF)
@@ -143,6 +159,8 @@
 
     lax.fori_loop(1, NT, a_start, 0)
 
+    for cp in fetch[5:]:
+        cp.wait()
     for i in range(ROWS):
         g = gate[:, i * B : (i + 1) * B].astype(F32)
         u = up[:, i * B : (i + 1) * B].astype(F32)
@@ -160,8 +178,8 @@
         keycol = jnp.where(block_of == n, v.astype(F32), keycol)
     keycol = (keycol + lax.rem(lane, 4).astype(F32))[0:1]
 
+    z_step(2)
     z_step(1)
-    z_step(2)
 
     def a_wait(s, carry):
         h = lax.rem(t + s, NT)
@@ -189,8 +207,8 @@
         cp.start()
         pend.append(cp)
 
+    z_step(4)
     z_step(3)
-    z_step(4)
 
     for k in (1, 3, 2):
         src = comm_x.at[lax.rem(x - k + NX, NX)]
@@ -296,6 +314,10 @@
         return carry
 
     lax.fori_loop(0, ROWS, hidden_grad, 0)
+    gg_out = pltpu.make_async_copy(gg, gg_hbm, out_sem.at[0])
+    gg_out.start()
+    ug_out = pltpu.make_async_copy(ug, ug_hbm, out_sem.at[1])
+    ug_out.start()
 
     for e in (0, 1):
         rx(e, 1, part.at[xi(1), 1 - e], fin_x.at[e, 1 - e]).wait_recv()
@@ -343,6 +365,9 @@
         v = yblock(0, h) + rcv_y[0, RY - 1, span[h], :].astype(F32) + rcv_y[1, RY - 1, span[h], :].astype(F32)
         wg[span[h], :] = v.astype(BF)
 
+    wg_out = pltpu.make_async_copy(wg, wg_hbm, out_sem.at[2])
+    wg_out.start()
+
     def a_done(s, carry):
         a_copy(s).wait_send()
         return carry
@@ -350,11 +375,12 @@
     lax.fori_loop(1, NT, a_done, 0)
     for cp in pend:
         cp.wait_send()
+    for cp in (gg_out, ug_out, wg_out):
+        cp.wait()
 
 
 def local(gate_pre, up_pre, out_grad, weight_slots, holder_blocks, holder_live_slots, row_columns):
-    vmem = pl.BlockSpec(memory_space=pltpu.VMEM)
-    smem = pl.BlockSpec(memory_space=pltpu.SMEM)
+    hbm = pl.BlockSpec(memory_space=pl.ANY)
     dma = pltpu.SemaphoreType.DMA
     gate_grad, up_grad, weight_grad = pl.pallas_call(
         kernel,
@@ -363,9 +389,12 @@
             jax.ShapeDtypeStruct(gate_pre.shape, BF),
             jax.ShapeDtypeStruct((NROW, B), BF),
         ),
-        in_specs=[vmem, vmem, vmem, pl.BlockSpec(memory_space=pl.ANY), smem, smem, smem],
-        out_specs=(vmem, vmem, vmem),
+        in_specs=[hbm] * 7,
+        out_specs=(hbm, hbm, hbm),
         scratch_shapes=[
+            pltpu.VMEM(gate_pre.shape, BF), pltpu.VMEM(up_pre.shape, BF), pltpu.VMEM(out_grad.shape, BF),
+            pltpu.SMEM((2, 3 * NT), jnp.int32), pltpu.SMEM((NT,), jnp.int32), pltpu.SMEM((ROWS, KEEP), jnp.int32),
+            pltpu.VMEM(gate_pre.shape, BF), pltpu.VMEM(gate_pre.shape, BF), pltpu.VMEM((NROW, B), BF),
             pltpu.VMEM((2 * NT, B, B), BF),
             pltpu.VMEM((3 * NT, 16, B), BF),
             pltpu.VMEM((NT, 16, B), BF),
@@ -382,7 +411,7 @@
             pltpu.VMEM((NY // 2, 2, NROW, B), F32),
             pltpu.VMEM((2, RY, NROW, B), BF),
             pltpu.VMEM((2, RY, NROW, B), BF),
-            dma,
+            dma((7,)), dma((3,)),
             dma((2, RZ, 2)), dma((2, RZ, 2)),
             dma((2, RZ + 1, 2)), dma((2, RZ + 1, 2)),
             dma((NT,)), dma((NT,)),
@@ -392,10 +421,10 @@
             dma((2, RY, 2)), dma((2, RY, 2)),
         ],
         compiler_params=pltpu.CompilerParams(
-            collective_id=0, has_side_effects=True, vmem_limit_bytes=40 * 1024 * 1024
+            collective_id=0, has_side_effects=True, vmem_limit_bytes=62 * 1024 * 1024
         ),
         cost_estimate=pl.CostEstimate(flops=600_000_000, bytes_accessed=4_000_000, transcendentals=82_000),
-    )(gate_pre, up_pre, out_grad, weight_slots, holder_blocks, holder_live_slots, row_columns)
+    )(gate_pre, up_pre, out_grad, weight_slots, holder_blocks.T, holder_live_slots, row_columns)
     return gate_grad, up_grad, weight_grad.reshape(ROWS * KEEP, 4 * B)
 
 

time: 92.6 us -> 85.7 us (0.925)
  the two profiles are of different devices: /device:TPU:10 before, /device:TPU:8 now
where the time goes in v2:
time: 85.7 us; the launch traced here: 85.4 us
  Pallas kernels  80.1 us (93%)
  local copies, waits for them, and re-layouts  4.7 us (5%)
    pallas_call x1, Pallas kernels, local(): pl.pallas_call(kernel, out_shape=(jax.ShapeDtypeStruct(gate_pre.shape, BF...  80.1 us
    unnamed x2, local copies, waits for them, and re-layouts  3.19 us

profile of v2, /device:TPU:8, one launch (start us, length us, event | category | flops | bytes accessed | tf_op | source)
XLA Modules:
  0.0 85.4 jit_solution(16100395646819323273)
XLA Ops:
  0.6 80.1 %shard_map.94 = (bf16[128,640]{1,0:T(8,128)(2,1)}, bf16[128,640]{1,0:T(8,128)(2,1)}, bf16[240,128]{1,0:T(8,128)(2,1)}) custom-call(bf16[128,640]{1,0:T(8,128)(2,1)} %gate_hbm.1, bf16[128,640]{1,0:T(8,128)(2,1)} %up_hbm.1, bf16[128,256]{1,0:T(8,128)(2,1)} %og_hbm.1, bf16[72,128,128]{2,1,0:T(8,128)(2,1)} %w_hbm.1, s32[2,72]{1,0:T(2,128)} %bitcast.1, ...), custom_call_target="tpu_custom_call" | custom-call | flops 600000000 | bytes 4000000 | tf_op jit(solution)/shard_map/pallas_call | solution.py:385
  80.7 1.5 %reshape.9 = bf16[60,512]{1,0:T(8,128)(2,1)} reshape(bf16[240,128]{1,0:T(8,128)(2,1)} %get-tuple-element.8) | data formatting | bytes 122880 | tf_op jit(solution)/shard_map/reshape | solution.py:428
  82.2 1.6 %copy.12 = bf16[128,640]{1,0:T(8,128)(2,1)} copy(bf16[128,640]{1,0:T(8,128)(2,1)} %get-tuple-element.12) | data formatting | bytes 327680
  83.8 1.6 %copy.13 = bf16[128,640]{1,0:T(8,128)(2,1)} copy(bf16[128,640]{1,0:T(8,128)(2,1)} %get-tuple-element.13) | data formatting | bytes 327680

commit v3 on v2

v3 whole, which is shorter than its diff:
```python
import jax
import jax.numpy as jnp
from jax import lax
from jax.experimental import pallas as pl
from jax.experimental.pallas import tpu as pltpu
from jax.sharding import PartitionSpec as P

MESH = pl.DeviceIdType.MESH
NX, NY, NZ = 4, 8, 12
NT = 2 * NZ
RZ, RY = NZ // 2, NY // 2
ROWS, KEEP, B = 5, 12, 128
HALF = KEEP // 2
TRI = 3 * B
BF, F32 = jnp.bfloat16, jnp.float32
NROW = ROWS * KEEP * 4
HROW = NROW // 2


def kernel(
    gate_hbm, up_hbm, og_hbm, w_hbm, hb_hbm, live_hbm, rc_hbm,
    gg_hbm, ug_hbm, wg_hbm,
    gate, up, og, hb, live, rc, gg, ug, wg,
    og_all, slab, msg, recv, comm_y, w_all, act, slope_up, hid_t, part_a, part_b,
    buf_x, fin_x, snd_x, far_y, near_y, one_y, two_y, snd_two, yin, snd_ya, rcv_ya, xin, snd_xb, rcv_xb, wgf,
    in_sem, out_sem, z_send, z_recv, s_send, s_recv, a_send, a_recv, gy_send, gy_recv, gx_send, gx_recv,
    rx_send, rx_recv, far_send, far_recv, near_send, near_recv, one_send, one_recv, two_send, two_recv,
    ya_send, ya_recv, xb_send, xb_recv,
):
    t, d = lax.axis_index("tensor"), lax.axis_index("dp")
    z, c = lax.div(t, 2), lax.rem(t, 2)
    x, y = lax.div(d, NY), lax.rem(d, NY)

    def zdev(k):
        return {"tensor": lax.rem(z + k + NZ, NZ) * 2 + c}

    def xdev(k):
        return {"dp": lax.rem(x + k + NX, NX) * NY + y}

    def ydev(k):
        return {"dp": x * NY + lax.rem(y + k + NY, NY)}

    sibling = {"tensor": z * 2 + (1 - c)}

    def copy(src, dst, ss, rs, dev):
        return pltpu.make_async_remote_copy(
            src_ref=src, dst_ref=dst, send_sem=ss, recv_sem=rs, device_id=dev, device_id_type=MESH
        )

    fetch = [
        pltpu.make_async_copy(src, dst, in_sem.at[n])
        for n, (src, dst) in enumerate([
            (og_hbm, og), (w_hbm.at[:, pl.ds(pl.multiple_of(x * 32 + lax.div(y, 4) * 16, 16), 16), :], slab), (hb_hbm, hb),
            (live_hbm, live), (rc_hbm, rc), (gate_hbm, gate), (up_hbm, up),
        ])
    ]
    for cp in fetch:
        cp.start()

    barrier = pltpu.get_barrier_semaphore()

    def greet(s, carry):
        pl.semaphore_signal(barrier, inc=1, device_id={"tensor": lax.rem(t + s, NT)}, device_id_type=MESH)
        return carry

    lax.fori_loop(1, NT, greet, 0)
    for k in (1, 2, 3):
        pl.semaphore_signal(barrier, inc=1, device_id=xdev(k), device_id_type=MESH)
    for k in range(1, NY):
        pl.semaphore_signal(barrier, inc=1, device_id=ydev(k), device_id_type=MESH)
    pend = []

    fetch[0].wait()
    og_all[2 * t] = og[:, :B]
    og_all[2 * t + 1] = og[:, B:]
    pl.semaphore_wait(barrier, NT - 1 + NX - 1 + NY - 1)

    def zslot(k, cc, h):
        return 2 * (lax.rem(z + k + NZ, NZ) * 2 + cc) + h

    class Ring:
        def __init__(self, radius, slot, dev, send, recv):
            self.radius, self.slot, self.dev, self.send, self.recv = radius, slot, dev, send, recv

        def chunks(self, s):
            return [(0, 0), (1, 1), (0, 1), (1, 0)][: 4 if s < self.radius else 2 if s == self.radius else 0]

        def copy(self, s, k, e, h):
            sg = 1 if e == 0 else -1
            slot = self.slot(-sg * s, h)
            return copy(slot, slot, self.send.at[e, s + k - 1, h], self.recv.at[e, s + k - 1, h], self.dev(sg * k))

        def start(self, s, e, h, ks=(2, 1)):
            for k in ks:
                if (e, h) in self.chunks(s + k):
                    cp = self.copy(s, k, e, h)
                    cp.start()
                    pend.append(cp)

        def open(self):
            for k in (2, 1):
                for e, h in self.chunks(1):
                    self.start(0, e, h, (k,))

        def step(self, s, arrived=None):
            for e, h in self.chunks(s):
                sg = 1 if e == 0 else -1
                slot = self.slot(-sg * s, h)
                copy(slot, slot, self.send.at[e, s - 1, h], self.recv.at[e, s - 1, h], self.dev(sg)).wait_recv()
                if s % 2 == 0:
                    self.start(s, e, h)
                if arrived is not None:
                    arrived(s, e, h)

    z_ring = Ring(RZ, lambda k, h: og_all.at[zslot(k, c, h)], zdev, z_send, z_recv)

    def sib_start(s, e, h):
        sg = 1 if e == 0 else -1
        slot = og_all.at[zslot(-sg * s, c, h)]
        cp = copy(slot, slot, s_send.at[e, s, h], s_recv.at[e, s, h], sibling)
        cp.start()
        pend.append(cp)

    def sib_wait(s, e, h):
        sg = 1 if e == 0 else -1
        slot = og_all.at[zslot(-sg * s, 1 - c, h)]
        copy(slot, slot, s_send.at[e, s, h], s_recv.at[e, s, h], sibling).wait_recv()

    def z_step(s):
        z_ring.step(s, sib_start)

    z_ring.open()
    for h in (0, 1):
        sib_start(0, 0, h)

    for cp in fetch[1:5]:
        cp.wait()
    r_out = lax.broadcasted_iota(jnp.int32, (64, 192), 0)
    r_in = lax.broadcasted_iota(jnp.int32, (64, 192), 1)
    q = lax.rem(r_out, 16)
    pick = (
        (lax.div(r_out, 16) == lax.div(r_in, 48))
        & (lax.div(q, 4) == lax.div(lax.rem(r_in, 48), 16))
        & (q < 12)
        & (lax.rem(y, 4) * 4 + lax.rem(q, 4) == lax.rem(r_in, 16))
    )
    pick = jnp.where(pick, 1.0, 0.0).astype(BF)
    row16 = lax.broadcasted_iota(jnp.int32, (16, B), 0)

    def make_msg(m, carry):
        rows = slab[pl.ds(m * 12, 12)].reshape(192, B)
        picked = jnp.dot(pick, rows, preferred_element_type=F32)
        for u in range(4):
            o = m * 4 + u
            tile = picked[16 * u : 16 * u + 16]
            for s in range(3):
                key = (hb[0, o * 3 + s] - o * ROWS) * 48 + hb[1, o * 3 + s]
                key = jnp.where(s < live[o], key, -1).astype(F32)
                tile = jnp.where(row16 == 12 + s, key, tile)
            msg[o] = tile.astype(BF)
        return carry

    lax.fori_loop(0, NT // 4, make_msg, 0)
    recv[t] = msg[t]

    def a_copy(s):
        o = lax.rem(t + s, NT)
        return copy(msg.at[o], recv.at[t], a_send.at[s], a_recv.at[t], {"tensor": o})

    def a_start(s, carry):
        a_copy(s).start()
        return carry

    lax.fori_loop(1, NT, a_start, 0)

    for cp in fetch[5:]:
        cp.wait()
    o_row = lax.broadcasted_iota(jnp.int32, (B, B), 0)
    o_col = lax.broadcasted_iota(jnp.int32, (B, B), 1)
    to_y = (
        (lax.div(o_row, 16) == lax.rem(lax.div(o_col, 4), NY))
        & (lax.rem(lax.div(o_row, 4), NX) == lax.div(o_col, 32))
        & (lax.rem(o_row, 4) == lax.rem(o_col, 4))
    )
    to_y = jnp.where(to_y, 1.0, 0.0).astype(BF)
    for i in range(ROWS):
        g = gate[:, i * B : (i + 1) * B].astype(F32)
        u = up[:, i * B : (i + 1) * B].astype(F32)
        sig = 1.0 / (1.0 + jnp.exp(-g))
        a = g * sig
        act[:, i * B : (i + 1) * B] = a
        slope_up[:, i * B : (i + 1) * B] = u * (sig * (1.0 + g * (1.0 - sig)))
        hid = (a * u).T.astype(BF)
        hid_t[0, i] = hid
        hid_t[1, i] = jnp.dot(to_y, hid, preferred_element_type=F32).astype(BF)

    lane = lax.broadcasted_iota(jnp.int32, (8, 2 * B), 1)
    block_of = lax.div(lane, 4)
    keycol = jnp.full((8, 2 * B), -100.0, F32)
    for n in range(ROWS * KEEP):
        v = ((n // KEEP) * 48 + rc[n // KEEP, n % KEEP]) * 4
        keycol = jnp.where(block_of == n, v.astype(F32), keycol)
    keycol = (keycol + lax.rem(lane, 4).astype(F32))[0:1]

    z_step(2)
    z_step(1)

    def a_wait(s, carry):
        h = lax.rem(t + s, NT)
        copy(msg.at[h], recv.at[h], a_send.at[s], a_recv.at[h], {"tensor": h}).wait_recv()
        return carry

    lax.fori_loop(1, NT, a_wait, 0)

    got = recv[...]
    gotf = got.astype(F32)
    rr = lax.broadcasted_iota(jnp.int32, (NT, 16, B), 1)
    keyrow = jnp.where(
        rr < 4, gotf[:, 12:13, :], jnp.where(rr < 8, gotf[:, 13:14, :], jnp.where(rr < 12, gotf[:, 14:15, :], -1000.0))
    )
    keyrow = (keyrow * 4.0 + lax.rem(rr, 4).astype(F32)).reshape(NT * 16, B)
    got = got.reshape(NT * 16, B)
    for v in range(2):
        hot = jnp.where(keyrow == keycol[:, v * B : (v + 1) * B], 1.0, 0.0).astype(BF)
        res = lax.dot_general(hot, got, (((0,), (0,)), ((), ())), preferred_element_type=F32).astype(BF)
        n_tiles = 8 if v == 0 else 7
        comm_y[y, 8 * v : 8 * v + n_tiles] = res[: 16 * n_tiles].reshape(n_tiles, 16, B)

    y_ring = Ring(
        RY,
        lambda k, h: comm_y.at[lax.rem(y + k + NY, NY), pl.ds(8 * h, 8 - h)],
        ydev, gy_send, gy_recv,
    )
    y_ring.open()

    z_step(4)
    z_step(3)
    y_ring.step(2)
    z_step(6)
    z_step(5)
    for h in (0, 1):
        sib_wait(0, 0, h)
    for s in range(1, RZ + 1):
        for e, h in z_ring.chunks(s):
            sib_wait(s, e, h)

    def products(half):
        def one(i, carry):
            for p in range(2):
                k = half * HALF + 3 * p
                three = jnp.concatenate([og_all[rc[i, k + m]] for m in range(3)], axis=1)
                res = jnp.dot(hid_t[half, i], three, preferred_element_type=F32).astype(BF)
                if half == 0:
                    part_a[:, p, i] = res.reshape(NX, 32, TRI)
                else:
                    part_b[:, p, i] = res.reshape(NY, 16, TRI)
            return carry

        lax.fori_loop(0, ROWS, one, 0)

    def xi(k):
        return lax.rem(x + k + NX, NX)

    def yi(k):
        return lax.rem(y + k + NY, NY)

    def rx(e, j, src, dst):
        return copy(src, dst, rx_send.at[e, j], rx_recv.at[e, j], xdev(1 if e == 0 else -1))

    def begin(cp):
        cp.start()
        pend.append(cp)

    def far(e):
        sg = 1 if e == 0 else -1
        return copy(part_b.at[yi(4), e], far_y.at[e], far_send.at[e], far_recv.at[e], ydev(2 * sg))

    def near(e, p):
        sg = 1 if e == 0 else -1
        return copy(part_b.at[yi(3 * sg), p], near_y.at[e, p], near_send.at[e, p], near_recv.at[e, p], ydev(sg))

    def one_hop(e, p):
        sg = 1 if e == 0 else -1
        return copy(part_b.at[yi(sg), p], one_y.at[e, p], one_send.at[e, p], one_recv.at[e, p], ydev(sg))

    def two_hops(e, p):
        sg = 1 if e == 0 else -1
        return copy(snd_two.at[e, p], two_y.at[e, p], two_send.at[e, p], two_recv.at[e, p], ydev(2 * sg))

    products(1)
    for e in (0, 1):
        begin(far(e))
    for p in (0, 1):
        for e in (0, 1):
            begin(near(e, e if p == 0 else 1 - e))
    products(0)
    begin(rx(0, 0, part_a.at[xi(2), 0], buf_x.at[0]))
    begin(rx(1, 0, part_a.at[xi(2), 1], buf_x.at[1]))
    begin(rx(0, 1, part_a.at[xi(1), 1], fin_x.at[0, 1]))
    begin(rx(1, 1, part_a.at[xi(-1), 0], fin_x.at[1, 0]))
    for p in (0, 1):
        for e in (0, 1):
            begin(one_hop(e, p))

    y_ring.step(1)
    y_ring.step(3)
    y_ring.step(4)
    swap = (
        (lax.div(o_row, 32) == lax.rem(lax.div(o_col, 4), 4))
        & (lax.rem(lax.div(o_row, 4), NY) == lax.div(o_col, 16))
        & (lax.rem(o_row, 4) == lax.rem(o_col, 4))
    )
    swap = jnp.where(swap, 1.0, 0.0).astype(BF)
    for g in range(15):
        res = jnp.dot(swap, comm_y[:, g].reshape(B, B), preferred_element_type=F32).astype(BF)
        for u in range(4):
            n = 4 * g + u
            i, k = n // KEEP, n % KEEP
            w_all[x, k // 3, i, :, (k % 3) * B : (k % 3 + 1) * B] = res[32 * u : 32 * u + 32]

    def gx(s, e, q, back):
        sg = 1 if e == 0 else -1
        slot = w_all.at[xi(-sg * back), q]
        return copy(slot, slot, gx_send.at[e, s - 1, q], gx_recv.at[e, s - 1, q], xdev(sg))

    x_all = [(0, 0), (1, 2), (0, 1), (1, 3), (0, 2), (1, 0), (0, 3), (1, 1)]
    for e, q in x_all:
        begin(gx(1, e, q, 0))

    for p in (0, 1):
        for e in (0, 1):
            q = 1 - e if p == 0 else e
            near(e, q).wait_recv()
            sg = 1 if e == 0 else -1
            v = part_b[yi(2 * sg), q].astype(F32) + near_y[e, q].astype(F32)
            if q == e:
                far(e).wait_recv()
                v = v + far_y[e].astype(F32)
            snd_two[e, q] = v.astype(BF)
            begin(two_hops(e, q))
    for e in (0, 1):
        rx(e, 0, part_a.at[xi(2), e], buf_x.at[e]).wait_recv()
        v = part_a[xi(1 if e == 0 else -1), e].astype(F32) + buf_x[e].astype(F32)
        snd_x[e] = v.astype(BF)
        begin(rx(e, 2, snd_x.at[e], fin_x.at[e, e]))

    for e, q in x_all:
        gx(1, e, q, 1).wait_recv()
        if (e, q) in x_all[:4]:
            begin(gx(2, e, q, 1))

    def scatter(own, groups, dst, i):
        low = lax.broadcasted_iota(jnp.int32, (groups, 8, B), 1) < 4
        own = own.reshape(groups, 8, HALF * B)
        for p in range(HALF // 2):
            a0 = own[:, :, 2 * p * B : (2 * p + 1) * B]
            a1 = own[:, :, (2 * p + 1) * B : (2 * p + 2) * B]
            first = (i * HALF + 2 * p) * 4
            dst[:, 0, first : first + 8, :] = jnp.where(low, a0, pltpu.roll(a1, 4, 1))
            dst[:, 1, first : first + 8, :] = jnp.where(low, pltpu.roll(a0, 4, 1), a1)

    for e in (0, 1):
        rx(e, 1, part_a.at[xi(1), 1 - e], fin_x.at[e, 1 - e]).wait_recv()
        rx(e, 2, snd_x.at[e], fin_x.at[e, e]).wait_recv()
    yin[:, :, HROW:, :] = jnp.zeros((NY // 2, 2, B - HROW, B), F32)
    for i in range(ROWS):
        own = [
            part_a[x, p, i].astype(F32) + fin_x[0, p, i].astype(F32) + fin_x[1, p, i].astype(F32) for p in (0, 1)
        ]
        scatter(jnp.concatenate(own, axis=1), NY // 2, yin, i)
    snd_ya[...] = yin[...].reshape(NY, B, B).astype(BF)

    def ya(k):
        return copy(snd_ya.at[yi(k)], rcv_ya.at[k - 1], ya_send.at[k - 1], ya_recv.at[k - 1], ydev(k))

    for k in (4, 3, 5, 2, 6, 1, 7):
        begin(ya(k))

    for e in (0, 1):
        for p in (0, 1):
            one_hop(e, p).wait_recv()
            two_hops(e, p).wait_recv()
    xin[:, :, HROW:, :] = jnp.zeros((NX // 2, 2, B - HROW, B), F32)
    for i in range(ROWS):
        own = [
            part_b[y, p, i].astype(F32) + one_y[0, p, i].astype(F32) + one_y[1, p, i].astype(F32)
            + two_y[0, p, i].astype(F32) + two_y[1, p, i].astype(F32)
            for p in (0, 1)
        ]
        scatter(jnp.concatenate(own, axis=1), NX // 2, xin, i)
    snd_xb[...] = xin[...].reshape(NX, B, B).astype(BF)

    def xb(k):
        return copy(snd_xb.at[xi(k)], rcv_xb.at[k - 1], xb_send.at[k - 1], xb_recv.at[k - 1], xdev(k))

    for k in (2, 1, 3):
        begin(xb(k))

    for e, q in x_all[:4]:
        gx(2, e, q, 2).wait_recv()

    def hidden_grad(i, carry):
        total = jnp.zeros((B, B), F32)
        for q in range(4):
            left = jnp.concatenate([og_all[rc[i, q * 3 + m]] for m in range(3)], axis=1)
            right = w_all[:, q, i].reshape(B, TRI)
            total = total + lax.dot_general(left, right, (((1,), (1,)), ((), ())), preferred_element_type=F32)
        cols = pl.ds(pl.multiple_of(i * B, B), B)
        gg[:, cols] = (total * slope_up[:, cols]).astype(BF)
        ug[:, cols] = (total * act[:, cols]).astype(BF)
        return carry

    lax.fori_loop(0, ROWS, hidden_grad, 0)
    gg_out = pltpu.make_async_copy(gg, gg_hbm, out_sem.at[0])
    gg_out.start()
    ug_out = pltpu.make_async_copy(ug, ug_hbm, out_sem.at[1])
    ug_out.start()

    for half, n, mine, box, cps in (
        (0, NY, yin[lax.div(y, 2), lax.rem(y, 2)], rcv_ya, ya),
        (1, NX, xin[lax.div(x, 2), lax.rem(x, 2)], rcv_xb, xb),
    ):
        for k in range(1, n):
            cps(k).wait_recv()
            mine = mine + box[k - 1].astype(F32)
        for i in range(ROWS):
            first = (i * KEEP + half * HALF) * 4
            wgf[first : first + 4 * HALF, :] = mine[i * 4 * HALF : (i + 1) * 4 * HALF]
    wg[...] = wgf[...].astype(BF)
    wg_out = pltpu.make_async_copy(wg, wg_hbm, out_sem.at[2])
    wg_out.start()

    def a_done(s, carry):
        a_copy(s).wait_send()
        return carry

    lax.fori_loop(1, NT, a_done, 0)
    for cp in pend:
        cp.wait_send()
    for cp in (gg_out, ug_out, wg_out):
        cp.wait()


def local(gate_pre, up_pre, out_grad, weight_slots, holder_blocks, holder_live_slots, row_columns):
    hbm = pl.BlockSpec(memory_space=pl.ANY)
    dma = pltpu.SemaphoreType.DMA
    gate_grad, up_grad, weight_grad = pl.pallas_call(
        kernel,
        out_shape=(
            jax.ShapeDtypeStruct(gate_pre.shape, BF),
            jax.ShapeDtypeStruct(gate_pre.shape, BF),
            jax.ShapeDtypeStruct((NROW, B), BF),
        ),
        in_specs=[hbm] * 7,
        out_specs=(hbm, hbm, hbm),
        scratch_shapes=[
            pltpu.VMEM(gate_pre.shape, BF), pltpu.VMEM(up_pre.shape, BF), pltpu.VMEM(out_grad.shape, BF),
            pltpu.SMEM((2, 3 * NT), jnp.int32), pltpu.SMEM((NT,), jnp.int32), pltpu.SMEM((ROWS, KEEP), jnp.int32),
            pltpu.VMEM(gate_pre.shape, BF), pltpu.VMEM(gate_pre.shape, BF), pltpu.VMEM((NROW, B), BF),
            pltpu.VMEM((2 * NT, B, B), BF),
            pltpu.VMEM((3 * NT, 16, B), BF),
            pltpu.VMEM((NT, 16, B), BF),
            pltpu.VMEM((NT, 16, B), BF),
            pltpu.VMEM((NY, 15, 16, B), BF),
            pltpu.VMEM((NX, 4, ROWS, 32, TRI), BF),
            pltpu.VMEM((B, ROWS * B), F32),
            pltpu.VMEM((B, ROWS * B), F32),
            pltpu.VMEM((2, ROWS, B, B), BF),
            pltpu.VMEM((NX, 2, ROWS, 32, TRI), BF),
            pltpu.VMEM((NY, 2, ROWS, 16, TRI), BF),
            pltpu.VMEM((2, ROWS, 32, TRI), BF),
            pltpu.VMEM((2, 2, ROWS, 32, TRI), BF),
            pltpu.VMEM((2, ROWS, 32, TRI), BF),
            pltpu.VMEM((2, ROWS, 16, TRI), BF),
            pltpu.VMEM((2, 2, ROWS, 16, TRI), BF),
            pltpu.VMEM((2, 2, ROWS, 16, TRI), BF),
            pltpu.VMEM((2, 2, ROWS, 16, TRI), BF),
            pltpu.VMEM((2, 2, ROWS, 16, TRI), BF),
            pltpu.VMEM((NY // 2, 2, B, B), F32),
            pltpu.VMEM((NY, B, B), BF), pltpu.VMEM((NY - 1, B, B), BF),
            pltpu.VMEM((NX // 2, 2, B, B), F32),
            pltpu.VMEM((NX, B, B), BF), pltpu.VMEM((NX - 1, B, B), BF),
            pltpu.VMEM((NROW, B), F32),
            dma((7,)), dma((3,)),
            dma((2, RZ, 2)), dma((2, RZ, 2)),
            dma((2, RZ + 1, 2)), dma((2, RZ + 1, 2)),
            dma((NT,)), dma((NT,)),
            dma((2, RY, 2)), dma((2, RY, 2)),
            dma((2, 2, 4)), dma((2, 2, 4)),
            dma((2, 3)), dma((2, 3)),
            dma((2,)), dma((2,)), dma((2, 2)), dma((2, 2)),
            dma((2, 2)), dma((2, 2)), dma((2, 2)), dma((2, 2)),
            dma((NY - 1,)), dma((NY - 1,)), dma((NX - 1,)), dma((NX - 1,)),
        ],
        compiler_params=pltpu.CompilerParams(
            collective_id=0, has_side_effects=True, vmem_limit_bytes=62 * 1024 * 1024
        ),
        cost_estimate=pl.CostEstimate(flops=600_000_000, bytes_accessed=4_000_000, transcendentals=82_000),
    )(gate_pre, up_pre, out_grad, weight_slots, holder_blocks.T, holder_live_slots, row_columns)
    return gate_grad, up_grad, weight_grad.reshape(ROWS * KEEP, 4 * B)


def solution(mesh):
    placed = (
        P("dp", "tensor"),
        P("dp", "tensor"),
        P("dp", "tensor"),
        P("tensor", None, None),
        P("tensor", None),
        P("tensor"),
        P("tensor", None),
    )
    return jax.shard_map(
        local,
        mesh=mesh,
        in_specs=placed,
        out_specs=(P("dp", "tensor"), P("dp", "tensor"), P("tensor", "dp")),
        check_vma=False,
    )
```

time: 85.7 us -> 79.5 us (0.928)
  the two profiles are of different devices: /device:TPU:8 before, /device:TPU:1 now
where the time goes in v3:
time: 79.5 us; the launch traced here: 79.3 us
  Pallas kernels  73.9 us (93%)
  local copies, waits for them, and re-layouts  4.7 us (6%)
    pallas_call x1, Pallas kernels, local(): pl.pallas_call(kernel, out_shape=(jax.ShapeDtypeStruct(gate_pre.shape, BF...  73.9 us
    unnamed x2, local copies, waits for them, and re-layouts  3.19 us

profile of v3, /device:TPU:1, one launch (start us, length us, event | category | flops | bytes accessed | tf_op | source)
XLA Modules:
  0.0 79.3 jit_solution(4243639181576424020)
XLA Ops:
  0.6 73.9 %shard_map.94 = (bf16[128,640]{1,0:T(8,128)(2,1)}, bf16[128,640]{1,0:T(8,128)(2,1)}, bf16[240,128]{1,0:T(8,128)(2,1)}) custom-call(bf16[128,640]{1,0:T(8,128)(2,1)} %gate_hbm.1, bf16[128,640]{1,0:T(8,128)(2,1)} %up_hbm.1, bf16[128,256]{1,0:T(8,128)(2,1)} %og_hbm.1, bf16[72,128,128]{2,1,0:T(8,128)(2,1)} %w_hbm.1, s32[2,72]{1,0:T(2,128)} %bitcast.1, ...), custom_call_target="tpu_custom_call" | custom-call | flops 600000000 | bytes 4000000 | tf_op jit(solution)/shard_map/pallas_call | solution.py:447
  74.6 1.5 %reshape.9 = bf16[60,512]{1,0:T(8,128)(2,1)} reshape(bf16[240,128]{1,0:T(8,128)(2,1)} %get-tuple-element.8) | data formatting | bytes 122880 | tf_op jit(solution)/shard_map/reshape | solution.py:500
  76.1 1.6 %copy.12 = bf16[128,640]{1,0:T(8,128)(2,1)} copy(bf16[128,640]{1,0:T(8,128)(2,1)} %get-tuple-element.12) | data formatting | bytes 327680
  77.7 1.6 %copy.13 = bf16[128,640]{1,0:T(8,128)(2,1)} copy(bf16[128,640]{1,0:T(8,128)(2,1)} %get-tuple-element.13) | data formatting | bytes 327680

commit v4 on v3

--- a/solution.py
+++ b/solution.py
@@ -21,9 +21,9 @@
     gate_hbm, up_hbm, og_hbm, w_hbm, hb_hbm, live_hbm, rc_hbm,
     gg_hbm, ug_hbm, wg_hbm,
     gate, up, og, hb, live, rc, gg, ug, wg,
-    og_all, slab, msg, recv, comm_y, w_all, act, slope_up, hid_t, part_a, part_b,
+    og_all, slab, msg, recv, comm_y, comm_x, w_all, w_b, act, slope_up, hid_t, part_a, part_b,
     buf_x, fin_x, snd_x, far_y, near_y, one_y, two_y, snd_two, yin, snd_ya, rcv_ya, xin, snd_xb, rcv_xb, wgf,
-    in_sem, out_sem, z_send, z_recv, s_send, s_recv, a_send, a_recv, gy_send, gy_recv, gx_send, gx_recv,
+    in_sem, out_sem, z_send, z_recv, s_send, s_recv, a_send, a_recv, gy_send, gy_recv, gx_send, gx_recv, c_send, c_recv, wy_send, wy_recv,
     rx_send, rx_recv, far_send, far_recv, near_send, near_recv, one_send, one_recv, two_send, two_recv,
     ya_send, ya_recv, xb_send, xb_recv,
 ):
@@ -168,10 +168,13 @@
         return copy(msg.at[o], recv.at[t], a_send.at[s], a_recv.at[t], {"tensor": o})
 
     def a_start(s, carry):
-        a_copy(s).start()
+        a_copy(lax.rem(s + NZ - 1, NT)).start()
         return carry
 
-    lax.fori_loop(1, NT, a_start, 0)
+    lax.fori_loop(1, NT // 2 + 1, a_start, 0)
+    lax.fori_loop(NT // 2 + 2, NT + 1, a_start, 0)
+
+    z_step(2)
 
     for cp in fetch[5:]:
         cp.wait()
@@ -198,12 +201,11 @@
     block_of = lax.div(lane, 4)
     keycol = jnp.full((8, 2 * B), -100.0, F32)
     for n in range(ROWS * KEEP):
-        v = ((n // KEEP) * 48 + rc[n // KEEP, n % KEEP]) * 4
+        i, k = (n // 8, n % 8) if n < 40 else ((n - 40) // 4, 8 + n % 4)
+        v = (i * 48 + rc[i, k]) * 4
         keycol = jnp.where(block_of == n, v.astype(F32), keycol)
     keycol = (keycol + lax.rem(lane, 4).astype(F32))[0:1]
 
-    z_step(2)
-    z_step(1)
 
     def a_wait(s, carry):
         h = lax.rem(t + s, NT)
@@ -223,19 +225,48 @@
     for v in range(2):
         hot = jnp.where(keyrow == keycol[:, v * B : (v + 1) * B], 1.0, 0.0).astype(BF)
         res = lax.dot_general(hot, got, (((0,), (0,)), ((), ())), preferred_element_type=F32).astype(BF)
-        n_tiles = 8 if v == 0 else 7
-        comm_y[y, 8 * v : 8 * v + n_tiles] = res[: 16 * n_tiles].reshape(n_tiles, 16, B)
+        if v == 0:
+            comm_y[y, 0:8] = res.reshape(8, 16, B)
+        else:
+            comm_y[y, 8:10] = res[:32].reshape(2, 16, B)
+            comm_x[x] = res[32:112].reshape(5, 16, B)
 
     y_ring = Ring(
         RY,
-        lambda k, h: comm_y.at[lax.rem(y + k + NY, NY), pl.ds(8 * h, 8 - h)],
+        lambda k, h: comm_y.at[lax.rem(y + k + NY, NY), pl.ds(5 * h, 5)],
         ydev, gy_send, gy_recv,
     )
+    wy_ring = Ring(RY, lambda k, h: w_b.at[lax.rem(y + k + NY, NY), h], ydev, wy_send, wy_recv)
+
+    def c_copy(k, back):
+        slot = comm_x.at[lax.rem(x - back + NX, NX)]
+        return copy(slot, slot, c_send.at[k - 1], c_recv.at[k - 1], xdev(k))
+
+    for k in (2, 1, 3):
+        cp = c_copy(k, 0)
+        cp.start()
+        pend.append(cp)
     y_ring.open()
 
     z_step(4)
+    for k in (1, 3, 2):
+        c_copy(k, k).wait_recv()
+    s_row = lax.broadcasted_iota(jnp.int32, (64, 64), 0)
+    s_col = lax.broadcasted_iota(jnp.int32, (64, 64), 1)
+    swap_x = (
+        (lax.div(s_row, 16) == lax.rem(lax.div(s_col, 4), 4))
+        & (lax.rem(lax.div(s_row, 4), NX) == lax.div(s_col, 16))
+        & (lax.rem(s_row, 4) == lax.rem(s_col, 4))
+    )
+    swap_x = jnp.where(swap_x, 1.0, 0.0).astype(BF)
+    for i in range(ROWS):
+        res = jnp.dot(swap_x, comm_x[:, i].reshape(64, B), preferred_element_type=F32).astype(BF)
+        for u in range(4):
+            w_b[y, u // 2, i, :, (u % 2) * B : (u % 2 + 1) * B] = res[16 * u : 16 * u + 16]
+    wy_ring.open()
+    y_ring.step(2)
+    z_step(1)
     z_step(3)
-    y_ring.step(2)
     z_step(6)
     z_step(5)
     for h in (0, 1):
@@ -302,6 +333,7 @@
         for e in (0, 1):
             begin(one_hop(e, p))
 
+    wy_ring.step(2)
     y_ring.step(1)
     y_ring.step(3)
     y_ring.step(4)
@@ -311,12 +343,12 @@
         & (lax.rem(o_row, 4) == lax.rem(o_col, 4))
     )
     swap = jnp.where(swap, 1.0, 0.0).astype(BF)
-    for g in range(15):
+    for g in range(10):
         res = jnp.dot(swap, comm_y[:, g].reshape(B, B), preferred_element_type=F32).astype(BF)
         for u in range(4):
             n = 4 * g + u
-            i, k = n // KEEP, n % KEEP
-            w_all[x, k // 3, i, :, (k % 3) * B : (k % 3 + 1) * B] = res[32 * u : 32 * u + 32]
+            i, k = n // 8, n % 8
+            w_all[x, k // 2, i, :, (k % 2) * B : (k % 2 + 1) * B] = res[32 * u : 32 * u + 32]
 
     def gx(s, e, q, back):
         sg = 1 if e == 0 else -1
@@ -399,11 +431,19 @@
     for e, q in x_all[:4]:
         gx(2, e, q, 2).wait_recv()
 
+    wy_ring.step(1)
+    wy_ring.step(3)
+    wy_ring.step(4)
+
     def hidden_grad(i, carry):
         total = jnp.zeros((B, B), F32)
-        for q in range(4):
-            left = jnp.concatenate([og_all[rc[i, q * 3 + m]] for m in range(3)], axis=1)
-            right = w_all[:, q, i].reshape(B, TRI)
+        for q in range(6):
+            left = jnp.concatenate([og_all[rc[i, q * 2 + m]] for m in range(2)], axis=1)
+            if q < 4:
+                right = w_all[:, q, i].reshape(B, 2 * B)
+            else:
+                right = w_b[:, q - 4, i].reshape(B, 2 * B)
+                right = jnp.dot(swap, right, preferred_element_type=F32).astype(BF)
             total = total + lax.dot_general(left, right, (((1,), (1,)), ((), ())), preferred_element_type=F32)
         cols = pl.ds(pl.multiple_of(i * B, B), B)
         gg[:, cols] = (total * slope_up[:, cols]).astype(BF)
@@ -426,7 +466,8 @@
         for i in range(ROWS):
             first = (i * KEEP + half * HALF) * 4
             wgf[first : first + 4 * HALF, :] = mine[i * 4 * HALF : (i + 1) * 4 * HALF]
-    wg[...] = wgf[...].astype(BF)
+    for a in range(4):
+        wg[:, a * B : (a + 1) * B] = wgf[pl.ds(a, ROWS * KEEP, stride=4), :].astype(BF)
     wg_out = pltpu.make_async_copy(wg, wg_hbm, out_sem.at[2])
     wg_out.start()
 
@@ -449,20 +490,22 @@
         out_shape=(
             jax.ShapeDtypeStruct(gate_pre.shape, BF),
             jax.ShapeDtypeStruct(gate_pre.shape, BF),
-            jax.ShapeDtypeStruct((NROW, B), BF),
+            jax.ShapeDtypeStruct((ROWS * KEEP, 4 * B), BF),
         ),
         in_specs=[hbm] * 7,
         out_specs=(hbm, hbm, hbm),
         scratch_shapes=[
             pltpu.VMEM(gate_pre.shape, BF), pltpu.VMEM(up_pre.shape, BF), pltpu.VMEM(out_grad.shape, BF),
             pltpu.SMEM((2, 3 * NT), jnp.int32), pltpu.SMEM((NT,), jnp.int32), pltpu.SMEM((ROWS, KEEP), jnp.int32),
-            pltpu.VMEM(gate_pre.shape, BF), pltpu.VMEM(gate_pre.shape, BF), pltpu.VMEM((NROW, B), BF),
+            pltpu.VMEM(gate_pre.shape, BF), pltpu.VMEM(gate_pre.shape, BF), pltpu.VMEM((ROWS * KEEP, 4 * B), BF),
             pltpu.VMEM((2 * NT, B, B), BF),
             pltpu.VMEM((3 * NT, 16, B), BF),
             pltpu.VMEM((NT, 16, B), BF),
             pltpu.VMEM((NT, 16, B), BF),
-            pltpu.VMEM((NY, 15, 16, B), BF),
-            pltpu.VMEM((NX, 4, ROWS, 32, TRI), BF),
+            pltpu.VMEM((NY, 10, 16, B), BF),
+            pltpu.VMEM((NX, 5, 16, B), BF),
+            pltpu.VMEM((NX, 4, ROWS, 32, 2 * B), BF),
+            pltpu.VMEM((NY, 2, ROWS, 16, 2 * B), BF),
             pltpu.VMEM((B, ROWS * B), F32),
             pltpu.VMEM((B, ROWS * B), F32),
             pltpu.VMEM((2, ROWS, B, B), BF),
@@ -487,6 +530,7 @@
             dma((NT,)), dma((NT,)),
             dma((2, RY, 2)), dma((2, RY, 2)),
             dma((2, 2, 4)), dma((2, 2, 4)),
+            dma((NX - 1,)), dma((NX - 1,)), dma((2, RY, 2)), dma((2, RY, 2)),
             dma((2, 3)), dma((2, 3)),
             dma((2,)), dma((2,)), dma((2, 2)), dma((2, 2)),
             dma((2, 2)), dma((2, 2)), dma((2, 2)), dma((2, 2)),
@@ -497,7 +541,7 @@
         ),
         cost_estimate=pl.CostEstimate(flops=600_000_000, bytes_accessed=4_000_000, transcendentals=82_000),
     )(gate_pre, up_pre, out_grad, weight_slots, holder_blocks.T, holder_live_slots, row_columns)
-    return gate_grad, up_grad, weight_grad.reshape(ROWS * KEEP, 4 * B)
+    return gate_grad, up_grad, weight_grad
 
 
 def solution(mesh):

time: 79.5 us -> 74.8 us (0.941)
  Pallas kernels: 73.9 us -> 68.6 us
    pallas_call x1, Pallas kernels: 73.9 us -> 68.6 us  [local(): pl.pallas_call(kernel, out_shape=(jax.ShapeDtypeStruct(gate_pre.shape, BF...]
    reshape x1 -> x0, local copies, waits for them, and re-layouts: 1.5 us -> none  [local(): return (gate_grad, up_grad, weight_grad.reshape(ROWS * KEEP, 4 * B))]
    unnamed x2 -> x3, local copies, waits for them, and re-layouts: 3.19 us -> 4.66 us
where the time goes in v4:
time: 74.8 us; the launch traced here: 74 us
  Pallas kernels  68.6 us (92%)
  local copies, waits for them, and re-layouts  4.66 us (6%)
    pallas_call x1, Pallas kernels, local(): pl.pallas_call(kernel, out_shape=(jax.ShapeDtypeStruct(gate_pre.shape, BF...  68.6 us
    unnamed x3, local copies, waits for them, and re-layouts  4.66 us

profile of v4, /device:TPU:1, one launch (start us, length us, event | category | flops | bytes accessed | tf_op | source)
XLA Modules:
  0.0 74.0 jit_solution(17952171929209956087)
XLA Ops:
  0.6 68.6 %shard_map.94 = (bf16[128,640]{1,0:T(8,128)(2,1)}, bf16[128,640]{1,0:T(8,128)(2,1)}, bf16[60,512]{1,0:T(8,128)(2,1)}) custom-call(bf16[128,640]{1,0:T(8,128)(2,1)} %gate_hbm.1, bf16[128,640]{1,0:T(8,128)(2,1)} %up_hbm.1, bf16[128,256]{1,0:T(8,128)(2,1)} %og_hbm.1, bf16[72,128,128]{2,1,0:T(8,128)(2,1)} %w_hbm.1, s32[2,72]{1,0:T(2,128)} %bitcast.1, ...), custom_call_target="tpu_custom_call" | custom-call | flops 600000000 | bytes 4000000 | tf_op jit(solution)/shard_map/pallas_call | solution.py:488
  69.3 1.6 %copy.13 = bf16[128,640]{1,0:T(8,128)(2,1)} copy(bf16[128,640]{1,0:T(8,128)(2,1)} %get-tuple-element.6) | data formatting | bytes 327680
  70.9 1.6 %copy.14 = bf16[128,640]{1,0:T(8,128)(2,1)} copy(bf16[128,640]{1,0:T(8,128)(2,1)} %get-tuple-element.7) | data formatting | bytes 327680
  72.5 1.5 %copy.15 = bf16[60,512]{1,0:T(8,128)(2,1)} copy(bf16[60,512]{1,0:T(8,128)(2,1)} %get-tuple-element.8) | data formatting | bytes 122880

commit v5 on v4

--- a/solution.py
+++ b/solution.py
@@ -19,9 +19,9 @@
 
 def kernel(
     gate_hbm, up_hbm, og_hbm, w_hbm, hb_hbm, live_hbm, rc_hbm,
-    gg_hbm, ug_hbm, wg_hbm,
-    gate, up, og, hb, live, rc, gg, ug, wg,
-    og_all, slab, msg, recv, comm_y, comm_x, w_all, w_b, act, slope_up, hid_t, part_a, part_b,
+    hg_hbm, wg_hbm,
+    gate, up, og, hb, live, rc, hg, wg,
+    og_all, slab, msg, recv, comm_y, comm_x, w_all, w_b, hid_t, part_a, part_b,
     buf_x, fin_x, snd_x, far_y, near_y, one_y, two_y, snd_two, yin, snd_ya, rcv_ya, xin, snd_xb, rcv_xb, wgf,
     in_sem, out_sem, z_send, z_recv, s_send, s_recv, a_send, a_recv, gy_send, gy_recv, gx_send, gx_recv, c_send, c_recv, wy_send, wy_recv,
     rx_send, rx_recv, far_send, far_recv, near_send, near_recv, one_send, one_recv, two_send, two_recv,
@@ -191,8 +191,6 @@
         u = up[:, i * B : (i + 1) * B].astype(F32)
         sig = 1.0 / (1.0 + jnp.exp(-g))
         a = g * sig
-        act[:, i * B : (i + 1) * B] = a
-        slope_up[:, i * B : (i + 1) * B] = u * (sig * (1.0 + g * (1.0 - sig)))
         hid = (a * u).T.astype(BF)
         hid_t[0, i] = hid
         hid_t[1, i] = jnp.dot(to_y, hid, preferred_element_type=F32).astype(BF)
@@ -446,15 +444,12 @@
                 right = jnp.dot(swap, right, preferred_element_type=F32).astype(BF)
             total = total + lax.dot_general(left, right, (((1,), (1,)), ((), ())), preferred_element_type=F32)
         cols = pl.ds(pl.multiple_of(i * B, B), B)
-        gg[:, cols] = (total * slope_up[:, cols]).astype(BF)
-        ug[:, cols] = (total * act[:, cols]).astype(BF)
+        hg[:, cols] = total
         return carry
 
     lax.fori_loop(0, ROWS, hidden_grad, 0)
-    gg_out = pltpu.make_async_copy(gg, gg_hbm, out_sem.at[0])
-    gg_out.start()
-    ug_out = pltpu.make_async_copy(ug, ug_hbm, out_sem.at[1])
-    ug_out.start()
+    hg_out = pltpu.make_async_copy(hg, hg_hbm, out_sem.at[0])
+    hg_out.start()
 
     for half, n, mine, box, cps in (
         (0, NY, yin[lax.div(y, 2), lax.rem(y, 2)], rcv_ya, ya),
@@ -468,7 +463,7 @@
             wgf[first : first + 4 * HALF, :] = mine[i * 4 * HALF : (i + 1) * 4 * HALF]
     for a in range(4):
         wg[:, a * B : (a + 1) * B] = wgf[pl.ds(a, ROWS * KEEP, stride=4), :].astype(BF)
-    wg_out = pltpu.make_async_copy(wg, wg_hbm, out_sem.at[2])
+    wg_out = pltpu.make_async_copy(wg, wg_hbm, out_sem.at[1])
     wg_out.start()
 
     def a_done(s, carry):
@@ -478,26 +473,25 @@
     lax.fori_loop(1, NT, a_done, 0)
     for cp in pend:
         cp.wait_send()
-    for cp in (gg_out, ug_out, wg_out):
+    for cp in (hg_out, wg_out):
         cp.wait()
 
 
 def local(gate_pre, up_pre, out_grad, weight_slots, holder_blocks, holder_live_slots, row_columns):
     hbm = pl.BlockSpec(memory_space=pl.ANY)
     dma = pltpu.SemaphoreType.DMA
-    gate_grad, up_grad, weight_grad = pl.pallas_call(
+    hidden_grad, weight_grad = pl.pallas_call(
         kernel,
         out_shape=(
-            jax.ShapeDtypeStruct(gate_pre.shape, BF),
-            jax.ShapeDtypeStruct(gate_pre.shape, BF),
+            jax.ShapeDtypeStruct(gate_pre.shape, F32),
             jax.ShapeDtypeStruct((ROWS * KEEP, 4 * B), BF),
         ),
         in_specs=[hbm] * 7,
-        out_specs=(hbm, hbm, hbm),
+        out_specs=(hbm, hbm),
         scratch_shapes=[
             pltpu.VMEM(gate_pre.shape, BF), pltpu.VMEM(up_pre.shape, BF), pltpu.VMEM(out_grad.shape, BF),
             pltpu.SMEM((2, 3 * NT), jnp.int32), pltpu.SMEM((NT,), jnp.int32), pltpu.SMEM((ROWS, KEEP), jnp.int32),
-            pltpu.VMEM(gate_pre.shape, BF), pltpu.VMEM(gate_pre.shape, BF), pltpu.VMEM((ROWS * KEEP, 4 * B), BF),
+            pltpu.VMEM(gate_pre.shape, F32), pltpu.VMEM((ROWS * KEEP, 4 * B), BF),
             pltpu.VMEM((2 * NT, B, B), BF),
             pltpu.VMEM((3 * NT, 16, B), BF),
             pltpu.VMEM((NT, 16, B), BF),
@@ -506,8 +500,6 @@
             pltpu.VMEM((NX, 5, 16, B), BF),
             pltpu.VMEM((NX, 4, ROWS, 32, 2 * B), BF),
             pltpu.VMEM((NY, 2, ROWS, 16, 2 * B), BF),
-            pltpu.VMEM((B, ROWS * B), F32),
-            pltpu.VMEM((B, ROWS * B), F32),
             pltpu.VMEM((2, ROWS, B, B), BF),
             pltpu.VMEM((NX, 2, ROWS, 32, TRI), BF),
             pltpu.VMEM((NY, 2, ROWS, 16, TRI), BF),
@@ -524,7 +516,7 @@
             pltpu.VMEM((NX // 2, 2, B, B), F32),
             pltpu.VMEM((NX, B, B), BF), pltpu.VMEM((NX - 1, B, B), BF),
             pltpu.VMEM((NROW, B), F32),
-            dma((7,)), dma((3,)),
+            dma((7,)), dma((2,)),
             dma((2, RZ, 2)), dma((2, RZ, 2)),
             dma((2, RZ + 1, 2)), dma((2, RZ + 1, 2)),
             dma((NT,)), dma((NT,)),
@@ -541,6 +533,10 @@
         ),
         cost_estimate=pl.CostEstimate(flops=600_000_000, bytes_accessed=4_000_000, transcendentals=82_000),
     )(gate_pre, up_pre, out_grad, weight_slots, holder_blocks.T, holder_live_slots, row_columns)
+    g, u = gate_pre.astype(F32), up_pre.astype(F32)
+    sig = jax.nn.sigmoid(g)
+    gate_grad = (hidden_grad * u * (sig * (1.0 + g * (1.0 - sig)))).astype(BF)
+    up_grad = (hidden_grad * (g * sig)).astype(BF)
     return gate_grad, up_grad, weight_grad
 
 

time: 74.8 us -> 73.6 us (0.984)
  local copies, waits for them, and re-layouts: 4.66 us -> 1.48 us
  other arithmetic: 0 us -> 1.87 us
    unnamed x3 -> x5, local copies, waits for them, and re-layouts: 4.66 us -> 1.48 us
    convert_element_type x0 -> x1, other arithmetic: none -> 1.87 us  [local(): up_grad = (hidden_grad * (g * sig)).astype(BF)]
where the time goes in v5:
time: 73.6 us; the launch traced here: 72.8 us
  Pallas kernels  68.8 us (93%)
  other arithmetic  1.87 us (3%)
  local copies, waits for them, and re-layouts  1.48 us (2%)
    pallas_call x1, Pallas kernels, local(): pl.pallas_call(kernel, out_shape=(jax.ShapeDtypeStruct(gate_pre.shape, F3...  68.8 us
    convert_element_type x1, other arithmetic, local(): up_grad = (hidden_grad * (g * sig)).astype(BF)  1.87 us
    unnamed x5, local copies, waits for them, and re-layouts  1.48 us

profile of v5, /device:TPU:1, one launch (start us, length us, event | category | flops | bytes accessed | tf_op | source)
XLA Modules:
  0.0 72.8 jit_solution(15141537003948661049)
XLA Ops:
  0.6 0.0 copy-start.1
  0.6 0.0 copy-start
  0.7 68.8 %shard_map.94 = (f32[128,640]{1,0:T(8,128)}, bf16[60,512]{1,0:T(8,128)(2,1)}) custom-call(bf16[128,640]{1,0:T(8,128)(2,1)} %gate_hbm.1, bf16[128,640]{1,0:T(8,128)(2,1)} %up_hbm.1, bf16[128,256]{1,0:T(8,128)(2,1)} %og_hbm.1, bf16[72,128,128]{2,1,0:T(8,128)(2,1)} %w_hbm.1, s32[2,72]{1,0:T(2,128)} %bitcast.1, s32[24]{0:T(128)} %live_hbm.1, s32[5,12]{1,0:T(8,128)} %rc_hbm.1), custom_call_target="tpu_custom_call" | custom-call | flops 600000000 | bytes 4000000 | tf_op jit(solution)/shard_map/pallas_call | solution.py:483
  69.4 0.0 copy-done.1
  69.4 0.0 copy-done
  69.4 1.9 %fusion.8 = (bf16[128,640]{1,0:T(8,128)(2,1)}, bf16[128,640]{1,0:T(8,128)(2,1)}) fusion(f32[128,640]{1,0:T(8,128)} %get-tuple-element.5, bf16[128,640]{1,0:T(8,128)(2,1)S(1)} %copy-done, bf16[128,640]{1,0:T(8,128)(2,1)S(1)} %copy-done.1), kind=kLoop, calls=%fused_computation.11 | loop fusion | flops 1228800 | bytes 983040 | tf_op jit(solution)/shard_map/convert_element_type | solution.py:539
  71.3 1.5 %copy.11 = bf16[60,512]{1,0:T(8,128)(2,1)} copy(bf16[60,512]{1,0:T(8,128)(2,1)} %get-tuple-element.14) | data formatting | bytes 122880
Async XLA Ops:
  0.6 68.8 %copy-start.1 = (bf16[128,640]{1,0:T(8,128)(2,1)S(1)}, bf16[128,640]{1,0:T(8,128)(2,1)}, u32[]{:S(2)}) copy-start(bf16[128,640]{1,0:T(8,128)(2,1)} %up_hbm.1) | copy-start | bytes 491524
  0.6 68.8 %copy-start = (bf16[128,640]{1,0:T(8,128)(2,1)S(1)}, bf16[128,640]{1,0:T(8,128)(2,1)}, u32[]{:S(2)}) copy-start(bf16[128,640]{1,0:T(8,128)(2,1)} %gate_hbm.1) | copy-start | bytes 491524

commit v6 on v5

--- a/solution.py
+++ b/solution.py
@@ -79,7 +79,8 @@
         return 2 * (lax.rem(z + k + NZ, NZ) * 2 + cc) + h
 
     class Ring:
-        def __init__(self, radius, slot, dev, send, recv):
+        def __init__(self, radius, slot, dev, send, recv, ks=(2, 1)):
+            self.ks = ks
             self.radius, self.slot, self.dev, self.send, self.recv = radius, slot, dev, send, recv
 
         def chunks(self, s):
@@ -90,7 +91,7 @@
             slot = self.slot(-sg * s, h)
             return copy(slot, slot, self.send.at[e, s + k - 1, h], self.recv.at[e, s + k - 1, h], self.dev(sg * k))
 
-        def start(self, s, e, h, ks=(2, 1)):
+        def start(self, s, e, h, ks):
             for k in ks:
                 if (e, h) in self.chunks(s + k):
                     cp = self.copy(s, k, e, h)
@@ -98,7 +99,7 @@
                     pend.append(cp)
 
         def open(self):
-            for k in (2, 1):
+            for k in self.ks:
                 for e, h in self.chunks(1):
                     self.start(0, e, h, (k,))
 
@@ -107,8 +108,8 @@
                 sg = 1 if e == 0 else -1
                 slot = self.slot(-sg * s, h)
                 copy(slot, slot, self.send.at[e, s - 1, h], self.recv.at[e, s - 1, h], self.dev(sg)).wait_recv()
-                if s % 2 == 0:
-                    self.start(s, e, h)
+                if s % len(self.ks) == 0:
+                    self.start(s, e, h, self.ks)
                 if arrived is not None:
                     arrived(s, e, h)
 
@@ -234,7 +235,7 @@
         lambda k, h: comm_y.at[lax.rem(y + k + NY, NY), pl.ds(5 * h, 5)],
         ydev, gy_send, gy_recv,
     )
-    wy_ring = Ring(RY, lambda k, h: w_b.at[lax.rem(y + k + NY, NY), h], ydev, wy_send, wy_recv)
+    wy_ring = Ring(RY, lambda k, h: w_b.at[lax.rem(y + k + NY, NY), h], ydev, wy_send, wy_recv, (1,))
 
     def c_copy(k, back):
         slot = comm_x.at[lax.rem(x - back + NX, NX)]
@@ -331,7 +332,7 @@
         for e in (0, 1):
             begin(one_hop(e, p))
 
-    wy_ring.step(2)
+    wy_ring.step(1)
     y_ring.step(1)
     y_ring.step(3)
     y_ring.step(4)
@@ -356,6 +357,7 @@
     x_all = [(0, 0), (1, 2), (0, 1), (1, 3), (0, 2), (1, 0), (0, 3), (1, 1)]
     for e, q in x_all:
         begin(gx(1, e, q, 0))
+    wy_ring.step(2)
 
     for p in (0, 1):
         for e in (0, 1):
@@ -373,11 +375,7 @@
         v = part_a[xi(1 if e == 0 else -1), e].astype(F32) + buf_x[e].astype(F32)
         snd_x[e] = v.astype(BF)
         begin(rx(e, 2, snd_x.at[e], fin_x.at[e, e]))
-
-    for e, q in x_all:
-        gx(1, e, q, 1).wait_recv()
-        if (e, q) in x_all[:4]:
-            begin(gx(2, e, q, 1))
+    wy_ring.step(3)
 
     def scatter(own, groups, dst, i):
         low = lax.broadcasted_iota(jnp.int32, (groups, 8, B), 1) < 4
@@ -405,6 +403,12 @@
 
     for k in (4, 3, 5, 2, 6, 1, 7):
         begin(ya(k))
+
+    for e, q in x_all:
+        gx(1, e, q, 1).wait_recv()
+        if (e, q) in x_all[:4]:
+            begin(gx(2, e, q, 1))
+
 
     for e in (0, 1):
         for p in (0, 1):
@@ -429,8 +433,6 @@
     for e, q in x_all[:4]:
         gx(2, e, q, 2).wait_recv()
 
-    wy_ring.step(1)
-    wy_ring.step(3)
     wy_ring.step(4)
 
     def hidden_grad(i, carry):

time: 73.6 us -> 73.4 us (level)
  no operation moved by 1% of the time
where the time goes in v6:
time: 73.4 us; the launch traced here: 73.2 us
  Pallas kernels  69.1 us (94%)
  other arithmetic  1.87 us (3%)
  local copies, waits for them, and re-layouts  1.48 us (2%)
    pallas_call x1, Pallas kernels, local(): pl.pallas_call(kernel, out_shape=(jax.ShapeDtypeStruct(gate_pre.shape, F3...  69.1 us
    convert_element_type x1, other arithmetic, local(): up_grad = (hidden_grad * (g * sig)).astype(BF)  1.87 us
    unnamed x5, local copies, waits for them, and re-layouts  1.48 us

profile of v6, /device:TPU:1, one launch (start us, length us, event | category | flops | bytes accessed | tf_op | source)
XLA Modules:
  0.0 73.2 jit_solution(6902601902724174275)
XLA Ops:
  0.6 0.0 copy-start.1
  0.6 0.0 copy-start
  0.7 69.1 %shard_map.94 = (f32[128,640]{1,0:T(8,128)}, bf16[60,512]{1,0:T(8,128)(2,1)}) custom-call(bf16[128,640]{1,0:T(8,128)(2,1)} %gate_hbm.1, bf16[128,640]{1,0:T(8,128)(2,1)} %up_hbm.1, bf16[128,256]{1,0:T(8,128)(2,1)} %og_hbm.1, bf16[72,128,128]{2,1,0:T(8,128)(2,1)} %w_hbm.1, s32[2,72]{1,0:T(2,128)} %bitcast.1, s32[24]{0:T(128)} %live_hbm.1, s32[5,12]{1,0:T(8,128)} %rc_hbm.1), custom_call_target="tpu_custom_call" | custom-call | flops 600000000 | bytes 4000000 | tf_op jit(solution)/shard_map/pallas_call | solution.py:485
  69.8 0.0 copy-done.1
  69.8 0.0 copy-done
  69.8 1.9 %fusion.8 = (bf16[128,640]{1,0:T(8,128)(2,1)}, bf16[128,640]{1,0:T(8,128)(2,1)}) fusion(f32[128,640]{1,0:T(8,128)} %get-tuple-element.5, bf16[128,640]{1,0:T(8,128)(2,1)S(1)} %copy-done, bf16[128,640]{1,0:T(8,128)(2,1)S(1)} %copy-done.1), kind=kLoop, calls=%fused_computation.11 | loop fusion | flops 1228800 | bytes 983040 | tf_op jit(solution)/shard_map/convert_element_type | solution.py:541
  71.7 1.5 %copy.11 = bf16[60,512]{1,0:T(8,128)(2,1)} copy(bf16[60,512]{1,0:T(8,128)(2,1)} %get-tuple-element.14) | data formatting | bytes 122880
Async XLA Ops:
  0.6 69.2 %copy-start.1 = (bf16[128,640]{1,0:T(8,128)(2,1)S(1)}, bf16[128,640]{1,0:T(8,128)(2,1)}, u32[]{:S(2)}) copy-start(bf16[128,640]{1,0:T(8,128)(2,1)} %up_hbm.1) | copy-start | bytes 491524
  0.6 69.2 %copy-start = (bf16[128,640]{1,0:T(8,128)(2,1)S(1)}, bf16[128,640]{1,0:T(8,128)(2,1)}, u32[]{:S(2)}) copy-start(bf16[128,640]{1,0:T(8,128)(2,1)} %gate_hbm.1) | copy-start | bytes 491524
